TPU v7x, 32 devices: a whole 2x2x4 slice. The times are simulated.
32 devices in a mesh: groups: 2 (over y), gx: 4 (over z), gy: 2 (over x), gz: 2 (over core).
Axes of the slice: x: 2, y: 2, z: 4, core: 2. Of those that a mesh axis runs over, the one named last changes fastest.
Arguments:
- tokens: bfloat16 [16, 8, 32, 128], P(('groups', 'gx'), 'gy', 'gz'), parts along dimension 0, may hold values from -6 to 6
- norm_gain: float32 [128], replicated, may hold values from 0.1 to 1.9
- project_weight: bfloat16 [128, 384], replicated, may hold values from -0.5 to 0.5
- output_weight: bfloat16 [128, 128], replicated, may hold values from -0.5 to 0.5
- position_bias: float32 [4, 125], replicated, may hold values from -3 to 333
- grad_output: bfloat16 [16, 8, 32, 128], P(('groups', 'gx'), 'gy', 'gz'), parts along dimension 0, may hold values from -6 to 6
Outputs:
- token_grad: float32 [16, 8, 32, 128], P(('groups', 'gx'), 'gy', 'gz'), parts along dimension 0
- project_grad: float32 [256, 384], P('groups'), parts along dimension 0
- output_grad: float32 [256, 128], P('groups'), parts along dimension 0
- gain_grad: float32 [256], P('groups'), parts along dimension 0
- bias_grad: float32 [8, 125], P('groups'), parts along dimension 0
There are 2 independent parts, one for each index of `groups`. A program takes and returns all parts, laid end to end along the dimension named above; an argument that names none is the same for every part. Nothing has to cross between parts.
All inputs are finite; a program needn't handle non-finite values.
Results may differ from a plain program's by a relative error of at most 0.0088.
Values may be sent and summed in bfloat16 or wider, within the bound.
A program may use at most 64 MiB of HBM per device.

v0:
```python
import jax
import jax.numpy as jnp
from jax import lax
from jax.sharding import PartitionSpec as P

WIN = 5


def with_halo(array, sides, width):
    for axis, dim in sides:
        size, length = (lax.axis_size(axis), array.shape[dim])
        up = [(i, (i + 1) % size) for i in range(size - 1)]
        down = [(j, i) for i, j in up]
        last = lax.slice_in_dim(array, length - width, length, axis=dim)
        leading = lax.slice_in_dim(array, 0, width, axis=dim)
        before = lax.ppermute(last, axis, up)
        after = lax.ppermute(leading, axis, down)
        array = jnp.concatenate([before, array, after], axis=dim)
    return array


def normalize(tokens, norm_gain):
    values = tokens.astype(jnp.float32)
    inverse = lax.rsqrt(jnp.mean(values * values, axis=-1, keepdims=True) + 1e-06)
    scaled = values * inverse
    return ((scaled * norm_gain).astype(jnp.bfloat16), scaled, inverse)


def fold_rims(padded, axis_dim, inner_len, radius):
    centre = lax.slice_in_dim(padded, 2 * radius, inner_len + 2 * radius, axis=axis_dim)
    lower_rim = lax.slice_in_dim(padded, 0, radius, axis=axis_dim)
    upper_rim = lax.slice_in_dim(
        padded, inner_len + 3 * radius, inner_len + 4 * radius, axis=axis_dim
    )
    lower_pad = [(0, 0)] * padded.ndim
    lower_pad[axis_dim] = (0, inner_len - radius)
    upper_pad = [(0, 0)] * padded.ndim
    upper_pad[axis_dim] = (inner_len - radius, 0)
    return centre + jnp.pad(lower_rim, lower_pad) + jnp.pad(upper_rim, upper_pad)


def fold_all(padded, inner_shape, radius):
    for axis_dim in range(3):
        padded = fold_rims(padded, axis_dim, inner_shape[axis_dim], radius)
    return padded


def inside_axis(device_index, cells, extent, radius):
    positions = device_index * cells + jnp.arange(cells + 2 * radius, dtype=jnp.int32) - radius
    return ((positions >= 0) & (positions < extent)).astype(jnp.float32)


def window_stack(source, pair_index, inner_shape):
    size_x, size_y, size_z = inner_shape
    along_x = pair_index // WIN
    along_y = pair_index % WIN
    rest = source.shape[3:]
    starts = (along_x, along_y, pair_index - pair_index) + tuple(
        (pair_index - pair_index for extra in rest)
    )
    part = lax.dynamic_slice(source, starts, (size_x, size_y, source.shape[2]) + rest)
    stacked = jnp.stack([part[:, :, shift : shift + size_z] for shift in range(WIN)])
    return stacked.reshape((WIN, size_x * size_y * size_z) + rest)


def expand_heads(values, head_size):
    return jnp.repeat(jnp.swapaxes(values, 1, 2), head_size, axis=2)


def head_sums(values, head_count):
    lead, rows, channels = values.shape
    return jnp.swapaxes(
        values.reshape(lead, rows, head_count, channels // head_count).sum(-1), 1, 2
    )


def attend_block(queries, key_values, inside_grid, position_bias, d_attended, inner_shape):
    size_x, size_y, size_z = inner_shape
    row_count = size_x * size_y * size_z
    channels = queries.shape[1]
    head_count = position_bias.shape[0]
    head_size = channels // head_count
    logit_scale = head_size ** (-0.5)
    pair_count = WIN * WIN
    first_turn = jnp.int32(0)
    last_turn = jnp.int32(pair_count)
    query_float = queries.astype(jnp.float32)
    grad_float = d_attended.astype(jnp.float32)

    def score_turn(pair_index, scores):
        stacked = window_stack(key_values, pair_index, inner_shape)
        keys = stacked[..., :channels].astype(jnp.float32)
        logits = head_sums(query_float[None] * keys, head_count) * logit_scale
        bias_cols = lax.dynamic_slice_in_dim(position_bias, pair_index * WIN, WIN, 1)
        logits = logits + bias_cols.T[:, :, None]
        allowed = window_stack(inside_grid, pair_index, inner_shape)[:, None, :]
        logits = jnp.where(allowed > 0, logits, -1e30)
        return lax.dynamic_update_index_in_dim(scores, logits, pair_index, 0)

    scores = lax.fori_loop(
        first_turn,
        last_turn,
        score_turn,
        jnp.zeros((pair_count, WIN, head_count, row_count), jnp.float32),
    )
    row_peak = jnp.max(scores, axis=(0, 1), keepdims=True)
    weights = jnp.exp(scores - row_peak)
    attn_probs = weights / jnp.sum(weights, axis=(0, 1), keepdims=True)
    probs_low = attn_probs.astype(jnp.bfloat16)

    def value_turn(pair_index, carry):
        running, prob_grads = carry
        stacked = window_stack(key_values, pair_index, inner_shape)
        values = stacked[..., channels:].astype(jnp.float32)
        probs_here = lax.dynamic_index_in_dim(probs_low, pair_index, 0, keepdims=False).astype(
            jnp.float32
        )
        running = running + jnp.sum(expand_heads(probs_here, head_size) * values, axis=0)
        grads_here = head_sums(grad_float[None] * values, head_count)
        return (running, lax.dynamic_update_index_in_dim(prob_grads, grads_here, pair_index, 0))

    start_values = (
        jnp.zeros((row_count, channels), jnp.float32),
        jnp.zeros(scores.shape, jnp.float32),
    )
    gathered, d_probs = lax.fori_loop(first_turn, last_turn, value_turn, start_values)
    attended = gathered.astype(jnp.bfloat16)
    centre = head_sums((grad_float * attended.astype(jnp.float32))[None], head_count)[None]
    d_scores = attn_probs * (d_probs - centre)
    bias_local = jnp.sum(d_scores, axis=3).reshape(WIN**3, head_count).T
    d_low = (d_scores * logit_scale).astype(jnp.bfloat16)
    pad_z = key_values.shape[2]

    def back_turn(pair_index, carry):
        d_query, d_pairs = carry
        stacked = window_stack(key_values, pair_index, inner_shape)
        keys = stacked[..., :channels].astype(jnp.float32)
        low_here = expand_heads(
            lax.dynamic_index_in_dim(d_low, pair_index, 0, keepdims=False).astype(jnp.float32),
            head_size,
        )
        probs_here = expand_heads(
            lax.dynamic_index_in_dim(probs_low, pair_index, 0, keepdims=False).astype(jnp.float32),
            head_size,
        )
        d_query = d_query + jnp.sum(low_here * keys, axis=0)
        update = jnp.concatenate(
            [low_here * query_float[None], probs_here * grad_float[None]], axis=-1
        )
        update = update.reshape(WIN, size_x, size_y, size_z, 2 * channels)
        slab = jnp.pad(update[0], ((0, 0), (0, 0), (0, pad_z - size_z), (0, 0)))
        for shift in range(1, WIN):
            slab = slab + jnp.pad(
                update[shift], ((0, 0), (0, 0), (shift, pad_z - size_z - shift), (0, 0))
            )
        along_x = pair_index // WIN
        along_y = pair_index % WIN
        anchor = pair_index - pair_index
        corner = (along_x, along_y, anchor, anchor)
        region = lax.dynamic_slice(d_pairs, corner, slab.shape)
        return (d_query, lax.dynamic_update_slice(d_pairs, region + slab, corner))

    pair_shape = key_values.shape[:3] + (2 * channels,)
    start_back = (jnp.zeros((row_count, channels), jnp.float32), jnp.zeros(pair_shape, jnp.float32))
    d_query, d_pairs = lax.fori_loop(first_turn, last_turn, back_turn, start_back)
    return (attended, d_query, d_pairs, bias_local)


def shards(tokens, norm_gain, project_weight, output_weight, position_bias, grad_output):
    size_x, size_y, size_z, channels = tokens.shape
    radius = WIN // 2
    row_count = size_x * size_y * size_z
    highest = lax.Precision.HIGHEST
    extent_x = size_x * lax.axis_size("gx")
    extent_y = size_y * lax.axis_size("gy")
    extent_z = size_z * lax.axis_size("gz")
    factor = (extent_x * extent_y * extent_z) ** (-0.5)
    inner_shape = (size_x, size_y, size_z)
    hidden, scaled, inverse = normalize(tokens, norm_gain)
    hidden_rows = hidden.reshape(row_count, channels)
    projected = jnp.dot(hidden_rows, project_weight, preferred_element_type=jnp.float32).astype(
        jnp.bfloat16
    )
    queries = projected[:, :channels]
    local_pairs = projected[:, channels:].reshape(size_x, size_y, size_z, 2 * channels)
    key_values = with_halo(local_pairs, (("gx", 0), ("gy", 1), ("gz", 2)), WIN // 2)
    inside_grid = (
        inside_axis(lax.axis_index("gx"), size_x, extent_x, radius)[:, None, None]
        * inside_axis(lax.axis_index("gy"), size_y, extent_y, radius)[None, :, None]
        * inside_axis(lax.axis_index("gz"), size_z, extent_z, radius)[None, None, :]
    )
    grad_rows = grad_output.reshape(row_count, channels)
    d_attended = jnp.einsum(
        "re,ce->rc", grad_rows, output_weight, preferred_element_type=jnp.float32
    ).astype(jnp.bfloat16)
    attended_rows, d_query, d_pairs, bias_local = attend_block(
        queries, key_values, inside_grid, position_bias, d_attended, inner_shape
    )
    output_local = jnp.einsum(
        "rc,re->ce", attended_rows, grad_rows, preferred_element_type=jnp.float32
    )
    weight_float = project_weight.astype(jnp.float32)
    hidden_float = hidden_rows.astype(jnp.float32)
    returned = with_halo(d_pairs, (("gx", 0), ("gy", 1), ("gz", 2)), WIN // 2)
    d_kv = fold_all(returned, inner_shape, radius).reshape(row_count, 2 * channels)
    d_project = jnp.concatenate([d_query, d_kv], axis=1)
    project_local = jnp.einsum("rc,re->ce", hidden_float, d_project, precision=highest)
    d_hidden = jnp.einsum("re,ce->rc", d_project, weight_float, precision=highest)
    scaled_rows = scaled.reshape(row_count, channels)
    inverse_rows = inverse.reshape(row_count, 1)
    gain_local = jnp.sum(d_hidden * scaled_rows, axis=0)
    d_scaled = d_hidden * norm_gain
    token_grad = inverse_rows * (
        d_scaled - scaled_rows * jnp.mean(d_scaled * scaled_rows, axis=-1, keepdims=True)
    )
    head_count = position_bias.shape[0]
    bucket = (
        jnp.concatenate(
            [
                project_local.reshape(-1),
                output_local.reshape(-1),
                gain_local,
                bias_local.reshape(-1),
            ]
        )
        * factor
    )
    summed = lax.psum(bucket, ("gx", "gy", "gz"))
    project_len = 3 * channels * channels
    output_len = channels * channels
    project_grad = summed[:project_len].reshape(channels, 3 * channels)
    output_grad = summed[project_len : project_len + output_len].reshape(channels, channels)
    gain_grad = summed[project_len + output_len : project_len + output_len + channels]
    bias_grad = summed[project_len + output_len + channels :].reshape(head_count, WIN**3)
    return (
        token_grad.reshape(size_x, size_y, size_z, channels),
        project_grad,
        output_grad,
        gain_grad,
        bias_grad,
    )


def solution(mesh):
    return jax.shard_map(
        shards,
        mesh=mesh,
        in_specs=(
            P(("groups", "gx"), "gy", "gz", None),
            P(),
            P(),
            P(),
            P(),
            P(("groups", "gx"), "gy", "gz", None),
        ),
        out_specs=(
            P(("groups", "gx"), "gy", "gz", None),
            P("groups", None),
            P("groups", None),
            P("groups"),
            P("groups", None),
        ),
        check_vma=False,
    )
```

profile of v0, /device:TPU:0, one launch (start us, length us, event | category | flops | bytes accessed | tf_op | source)
XLA Modules:
  0.0 316.6 jit_solution(10502022046736549877)
XLA Ops:
  9.2 1.3 collective-permute-start.1
  10.5 5.6 %collective-permute-start = (bf16[2,4,16,256]{3,2,1,0:T(8,128)(2,1)S(1)}, bf16[2,4,16,256]{3,2,1,0:T(8,128)(2,1)S(1)}, u32[]{:S(2)}, u32[]{:S(2)}) collective-permute-start(bf16[2,4,16,256]{3,2,1,0:T(8,128)(2,1)S(1)} %bitcast.182), channel_id=1, source_target_pairs={{0,4},{4,8},{8,12},{1,5},{5,9},{9,13},{2,6},{6,10},{10,14},{3,7},{... | collective-permute-start | bytes 196616 | tf_op jit(solution)/shard_map/ppermute | solution.py:16
  18.0 3.8 %collective-permute-start.2 = (bf16[6,2,16,256]{3,2,1,0:T(8,128)(2,1)S(1)}, bf16[6,2,16,256]{3,2,1,0:T(8,128)(2,1)S(1)}, u32[]{:S(2)}, u32[]{:S(2)}) collective-permute-start(bf16[6,2,16,256]{3,2,1,0:T(8,128)(2,1)S(1)} %get-tuple-element.467), channel_id=1, source_target_pairs={{0,2},{1,3},{4,6},{5,7},{8,10},{9,11},{12,14},{13,15},{16,18},{17,... | collective-permute-start | bytes 294920 | tf_op jit(solution)/shard_map/ppermute | solution.py:16
  21.8 1.3 collective-permute-start.3
  24.0 4.3 %collective-permute-done.3 = bf16[6,2,16,256]{3,2,1,0:T(8,128)(2,1)S(1)} collective-permute-done((bf16[6,2,16,256]{3,2,1,0:T(8,128)(2,1)S(1)}, bf16[6,2,16,256]{3,2,1,0:T(8,128)(2,1)S(1)}, u32[]{:S(2)}, u32[]{:S(2)}) %collective-permute-start.3) | collective-permute-done | bytes 98336 | tf_op jit(solution)/shard_map/ppermute | solution.py:17
  28.4 1.3 collective-permute-start.4
  29.7 1.3 collective-permute-start.5
  31.2 1.6 collective-permute-done.5
  33.3 31.6 %while.42 = (s32[]{:T(128)}, f32[25,5,4,128]{3,2,1,0:T(4,128)S(1)}, f32[6,8,20]{2,1,0:T(8,128)S(1)}, f32[128,128]{1,0:T(8,128)S(1)}, bf16[6,8,20,256]{3,2,1,0:T(...) while((s32[]{:T(128)}, f32[25,5,4,128]{3,2,1,0:T(4,128)S(1)}, ...), condition=%wide.region_3.4_spmd, body=%wide.region_1.3_spmd.sunk | while | flops 251548 | bytes 2906034 | solution.py:100
  65.3 26.1 %while.43 = (s32[]{:T(128)}, f32[128,128]{0,1:T(8,128)S(1)}, f32[25,5,4,128]{3,2,1,0:T(4,128)S(1)}, bf16[25,5,4,128]{3,2,1,0:T(4,128)(2,1)S(1)}, bf16[6,8,20,256...) while((s32[]{:T(128)}, f32[128,128]{0,1:T(8,128)S(1)}, ...), condition=%wide.region_9.10_spmd.clone, body=%wide.region_6.9_spmd.clone.sunk | while | flops 507929 | bytes 2678190 | solution.py:126
  92.4 80.1 %while.44 = (s32[]{:T(128)}, f32[128,128]{0,1:T(8,128)S(1)}, f32[6,8,20,256]{3,2,1,0:T(8,128)S(1)}, bf16[25,5,4,128]{3,2,1,0:T(4,128)(2,1)}, bf16[6,8,20,256]{3,...) while((s32[]{:T(128)}, f32[128,128]{0,1:T(8,128)S(1)}, ...), condition=%wide.region_13.14_spmd.clone, body=%wide.region_11.13_spmd.clone.sunk | while | flops 799769 | bytes 7924222 | solution.py:165
  172.5 4.3 %collective-permute-start.6 = (f32[2,8,20,256]{3,2,1,0:T(8,128)S(1)}, f32[2,8,20,256]{3,2,1,0:T(8,128)S(1)}, u32[]{:S(2)}, u32[]{:S(2)}) collective-permute-start(f32[2,8,20,256]{3,2,1,0:T(8,128)S(1)} %get-tuple-element.462), channel_id=1, source_target_pairs={{0,4},{4,8},{8,12},{1,5},{5,9},{9,13},{2,6},{6,10},{10,14},{3,7},{... | collective-permute-start | bytes 983048 | tf_op jit(solution)/shard_map/ppermute | solution.py:16
  176.8 1.3 collective-permute-start.7
  178.1 7.4 %collective-permute-done.6 = f32[2,8,20,256]{3,2,1,0:T(8,128)S(1)} collective-permute-done((f32[2,8,20,256]{3,2,1,0:T(8,128)S(1)}, f32[2,8,20,256]{3,2,1,0:T(8,128)S(1)}, u32[]{:S(2)}, u32[]{:S(2)}) %collective-permute-start.6) | collective-permute-done | bytes 327712 | tf_op jit(solution)/shard_map/ppermute | solution.py:16
  185.6 4.0 %collective-permute-done.7 = f32[2,8,20,256]{3,2,1,0:T(8,128)S(1)} collective-permute-done((f32[2,8,20,256]{3,2,1,0:T(8,128)S(1)}, f32[2,8,20,256]{3,2,1,0:T(8,128)S(1)}, u32[]{:S(2)}, u32[]{:S(2)}) %collective-permute-start.7) | collective-permute-done | bytes 327712 | tf_op jit(solution)/shard_map/ppermute | solution.py:17
  189.7 1.6 collective-permute-start.8
  191.3 1.3 collective-permute-start.9
  192.6 8.3 %collective-permute-done.8 = f32[10,2,20,256]{3,2,1,0:T(8,128)S(1)} collective-permute-done((f32[10,2,20,256]{3,2,1,0:T(8,128)S(1)}, f32[10,2,20,256]{3,2,1,0:T(8,128)S(1)}, u32[]{:S(2)}, u32[]{:S(2)}) %collective-permute-start.8) | collective-permute-done | bytes 409632 | tf_op jit(solution)/shard_map/ppermute | solution.py:16
  201.0 4.2 %collective-permute-done.9 = f32[10,2,20,256]{3,2,1,0:T(8,128)S(1)} collective-permute-done((f32[10,2,20,256]{3,2,1,0:T(8,128)S(1)}, f32[10,2,20,256]{3,2,1,0:T(8,128)S(1)}, u32[]{:S(2)}, u32[]{:S(2)}) %collective-permute-start.9) | collective-permute-done | bytes 409632 | tf_op jit(solution)/shard_map/ppermute | solution.py:17
  206.1 2.0 collective-permute-start.10
  208.1 1.3 collective-permute-start.11
  209.9 1.9 collective-permute-done.11
  216.5 87.6 %all-reduce.9.cloned.1.call-done = f32[66164]{0:T(1024)} async-done(((f32[66164]{0:T(1024)}), f32[66164]{0:T(1024)}) %all-reduce.9.cloned.1.call-update) | async-done | bytes 264672 | tf_op jit(solution)/shard_map/psum | solution.py:228
  308.3 1.5 slice_bitcast_fusion
  (1628 shorter events, 146.2 us)
Async XLA Ops:
  7.2 1.8 copy-start
  7.2 296.9 %all-reduce.9.cloned.1.call-start = ((), (), s32[]{:S(2)}) async-start(), calls=%async_computation | async-start | bytes 532480 | tf_op jit(solution)/shard_map/psum | solution.py:228
  9.0 8.1 %copy-start.1 = (bf16[2,4,16,128]{3,2,1,0:T(8,128)(2,1)}, bf16[2,4,16,128]{3,2,1,0:T(8,128)(2,1)S(1)}, u32[]{:S(2)}) copy-start(bf16[2,4,16,128]{3,2,1,0:T(8,128)(2,1)S(1)} %get-tuple-element.469) | copy-start | bytes 98308
  9.2 7.9 %collective-permute-start.1 = (bf16[2,4,16,256]{3,2,1,0:T(8,128)(2,1)S(1)}, bf16[2,4,16,256]{3,2,1,0:T(8,128)(2,1)S(1)}, u32[]{:S(2)}, u32[]{:S(2)}) collective-permute-start(bf16[2,4,16,256]{3,2,1,0:T(8,128)(2,1)S(1)} %bitcast.181), channel_id=1, source_target_pairs={{4,0},{8,4},{12,8},{5,1},{9,5},{13,9},{6,2},{10,6},{14,10},{7,3},{... | collective-permute-start | bytes 196616 | tf_op jit(solution)/shard_map/ppermute | solution.py:17
  10.5 7.5 %collective-permute-start = (bf16[2,4,16,256]{3,2,1,0:T(8,128)(2,1)S(1)}, bf16[2,4,16,256]{3,2,1,0:T(8,128)(2,1)S(1)}, u32[]{:S(2)}, u32[]{:S(2)}) collective-permute-start(bf16[2,4,16,256]{3,2,1,0:T(8,128)(2,1)S(1)} %bitcast.182), channel_id=1, source_target_pairs={{0,4},{4,8},{8,12},{1,5},{5,9},{9,13},{2,6},{6,10},{10,14},{3,7},{... | collective-permute-start | bytes 196616 | tf_op jit(solution)/shard_map/ppermute | solution.py:16
  18.0 15.3 %copy-start.6 = (f32[4,125]{1,0:T(4,128)S(1)}, f32[4,125]{1,0:T(4,128)}, u32[]{:S(2)}) copy-start(f32[4,125]{1,0:T(4,128)} %param.16) | copy-start | bytes 6004
  18.0 6.0 %collective-permute-start.2 = (bf16[6,2,16,256]{3,2,1,0:T(8,128)(2,1)S(1)}, bf16[6,2,16,256]{3,2,1,0:T(8,128)(2,1)S(1)}, u32[]{:S(2)}, u32[]{:S(2)}) collective-permute-start(bf16[6,2,16,256]{3,2,1,0:T(8,128)(2,1)S(1)} %get-tuple-element.467), channel_id=1, source_target_pairs={{0,2},{1,3},{4,6},{5,7},{8,10},{9,11},{12,14},{13,15},{16,18},{17,... | collective-permute-start | bytes 294920 | tf_op jit(solution)/shard_map/ppermute | solution.py:16
  21.8 6.5 %collective-permute-start.3 = (bf16[6,2,16,256]{3,2,1,0:T(8,128)(2,1)S(1)}, bf16[6,2,16,256]{3,2,1,0:T(8,128)(2,1)S(1)}, u32[]{:S(2)}, u32[]{:S(2)}) collective-permute-start(bf16[6,2,16,256]{3,2,1,0:T(8,128)(2,1)S(1)} %get-tuple-element.468), channel_id=1, source_target_pairs={{2,0},{3,1},{6,4},{7,5},{10,8},{11,9},{14,12},{15,13},{18,16},{19,... | collective-permute-start | bytes 294920 | tf_op jit(solution)/shard_map/ppermute | solution.py:17
  28.4 2.8 collective-permute-start.4
  29.7 3.1 collective-permute-start.5
  97.9 0.9 copy-start.4
  101.1 0.9 copy-start.4
  104.3 0.9 copy-start.4
  107.5 0.9 copy-start.4
  172.5 13.0 %collective-permute-start.6 = (f32[2,8,20,256]{3,2,1,0:T(8,128)S(1)}, f32[2,8,20,256]{3,2,1,0:T(8,128)S(1)}, u32[]{:S(2)}, u32[]{:S(2)}) collective-permute-start(f32[2,8,20,256]{3,2,1,0:T(8,128)S(1)} %get-tuple-element.462), channel_id=1, source_target_pairs={{0,4},{4,8},{8,12},{1,5},{5,9},{9,13},{2,6},{6,10},{10,14},{3,7},{... | collective-permute-start | bytes 983048 | tf_op jit(solution)/shard_map/ppermute | solution.py:16
  176.8 12.8 %collective-permute-start.7 = (f32[2,8,20,256]{3,2,1,0:T(8,128)S(1)}, f32[2,8,20,256]{3,2,1,0:T(8,128)S(1)}, u32[]{:S(2)}, u32[]{:S(2)}) collective-permute-start(f32[2,8,20,256]{3,2,1,0:T(8,128)S(1)} %get-tuple-element.461), channel_id=1, source_target_pairs={{4,0},{8,4},{12,8},{5,1},{9,5},{13,9},{6,2},{10,6},{14,10},{7,3},{... | collective-permute-start | bytes 983048 | tf_op jit(solution)/shard_map/ppermute | solution.py:17
  189.7 11.2 %collective-permute-start.8 = (f32[10,2,20,256]{3,2,1,0:T(8,128)S(1)}, f32[10,2,20,256]{3,2,1,0:T(8,128)S(1)}, u32[]{:S(2)}, u32[]{:S(2)}) collective-permute-start(f32[10,2,20,256]{3,2,1,0:T(8,128)S(1)} %get-tuple-element.459), channel_id=1, source_target_pairs={{0,2},{1,3},{4,6},{5,7},{8,10},{9,11},{12,14},{13,15},{16,18},{17,... | collective-permute-start | bytes 1228808 | tf_op jit(solution)/shard_map/ppermute | solution.py:16
  191.3 18.4 %copy-start.5 = (bf16[2,4,16,128]{3,2,1,0:T(8,128)(2,1)S(1)}, bf16[2,4,16,128]{3,2,1,0:T(8,128)(2,1)}, u32[]{:S(2)}) copy-start(bf16[2,4,16,128]{3,2,1,0:T(8,128)(2,1)} %param.17) | copy-start | bytes 98308
  191.3 13.8 %collective-permute-start.9 = (f32[10,2,20,256]{3,2,1,0:T(8,128)S(1)}, f32[10,2,20,256]{3,2,1,0:T(8,128)S(1)}, u32[]{:S(2)}, u32[]{:S(2)}) collective-permute-start(f32[10,2,20,256]{3,2,1,0:T(8,128)S(1)} %get-tuple-element.460), channel_id=1, source_target_pairs={{2,0},{3,1},{6,4},{7,5},{10,8},{11,9},{14,12},{15,13},{18,16},{19,... | collective-permute-start | bytes 1228808 | tf_op jit(solution)/shard_map/ppermute | solution.py:17
  206.1 3.8 %collective-permute-start.10 = (f32[10,12,2,256]{3,2,1,0:T(2,128)}, f32[10,12,2,256]{3,2,1,0:T(2,128)}, u32[]{:S(2)}, u32[]{:S(2)}) collective-permute-start(f32[10,12,2,256]{3,2,1,0:T(2,128)} %get-tuple-element.457), channel_id=1, source_target_pairs={{0,1},{2,3},{4,5},{6,7},{8,9},{10,11},{12,13},{14,15},{16,17},{18,... | collective-permute-start | bytes 737288 | tf_op jit(solution)/shard_map/ppermute | solution.py:16
  208.1 3.7 %collective-permute-start.11 = (f32[10,12,2,256]{3,2,1,0:T(2,128)}, f32[10,12,2,256]{3,2,1,0:T(2,128)}, u32[]{:S(2)}, u32[]{:S(2)}) collective-permute-start(f32[10,12,2,256]{3,2,1,0:T(2,128)} %get-tuple-element.458), channel_id=1, source_target_pairs={{1,0},{3,2},{5,4},{7,6},{9,8},{11,10},{13,12},{15,14},{17,16},{19,... | collective-permute-start | bytes 737288 | tf_op jit(solution)/shard_map/ppermute | solution.py:17
  212.7 1.3 copy-start.9
  212.7 1.4 copy-start.8
  212.7 1.5 copy-start.2
  (47 other events, 35.8 us)
Sparse Core Ops, SparseCore 0:
  215.9 88.1 all-reduce.8
where the time goes:
time: 319 us; the launch traced here: 317 us
  waiting for transfers between devices  121 us (38%)
  local copies, waits for them, and re-layouts  105 us (33%)
  other arithmetic  39.5 us (12%)
  starting transfers between devices  26.3 us (8%)
  between operations  14.5 us (5%)
  loops' own time  8.87 us (3%)
    psum x1, waiting for transfers between devices, shards(): summed = lax.psum(bucket, ('gx', 'gy', 'gz'))  87.6 us
    another operation x475, local copies, waits for them, and re-layouts, window_stack(): jnp.stack([part[:, :, shift:shift + size_z] for shift in range(WIN)])  41 us
    while x400, local copies, waits for them, and re-layouts  25.7 us
    ppermute x6, starting transfers between devices, with_halo(): before = lax.ppermute(last, axis, up)  18.5 us
    transpose x75, other arithmetic, expand_heads(): return jnp.repeat(jnp.swapaxes(values, 1, 2), head_size, axis=2)  17.7 us
    ppermute x6, waiting for transfers between devices, with_halo(): before = lax.ppermute(last, axis, up)  17.4 us
    ppermute x6, waiting for transfers between devices, with_halo(): after = lax.ppermute(leading, axis, down)  16 us
    slice x100, local copies, waits for them, and re-layouts, window_stack(): part[:, :, shift:shift + size_z]  10.7 us
  transfers between devices with their start and end apart: 13, of which 10 were waited for; matrix products, arithmetic and copies ran while one was open for 1% of the time, Pallas kernels for 0%

commit v1 on v0

v1 whole, which is shorter than its diff:
```python
import functools

import jax
import jax.numpy as jnp
from jax import lax
from jax.experimental import pallas as pl
from jax.experimental.pallas import tpu as pltpu
from jax.sharding import PartitionSpec as P

WIN = 5
RADIUS = 2
FAR = -1e30
BF = jnp.bfloat16
F32 = jnp.float32


def dot(a, b, over):
    return lax.dot_general(a, b, ((over[:1], over[1:]), ((), ())), preferred_element_type=F32)


def digits(index, steps):
    out = []
    for step, count in steps:
        digit = jnp.zeros_like(index)
        for i in range(1, count):
            digit = digit + (index >= step * i).astype(jnp.int32)
        index = index - digit * step
        out.append(digit)
    return out


def one_hot(dims, lanes):
    _, pad_y, pad_z = dims
    rows = lax.broadcasted_iota(jnp.int32, (128, 1), 0)
    i, j, l = digits(rows, ((WIN * WIN, WIN + 1), (WIN, WIN), (1, WIN)))
    code = jnp.where(rows < WIN**3, (i * pad_y + j) * pad_z + l, -1)
    return (lax.broadcasted_iota(jnp.int32, (128, lanes), 1) == code).astype(F32)


def bias_table(bias_ref, spread, table, inner, dims, lanes, extents):
    heads = bias_ref.shape[0]
    size_x, size_y, size_z = inner
    pad_x, pad_y, pad_z = dims
    spread[...] = jnp.zeros_like(spread)
    spread[0:heads, 0 : WIN**3] = bias_ref[...]
    base = lax.dot_general(
        spread[...],
        one_hot(dims, lanes),
        (((1,), (0,)), ((), ())),
        precision=lax.Precision.HIGHEST,
        preferred_element_type=F32,
    )
    lane = lax.broadcasted_iota(jnp.int32, (1, lanes), 1)
    at = digits(lane, ((pad_y * pad_z, pad_x + 2), (pad_z, pad_y), (1, pad_z)))
    near = (at[0] < WIN) & (at[1] < WIN) & (at[2] < WIN)
    base = jnp.where(near, base, FAR)
    valid = lane < pad_x * pad_y * pad_z
    for digit, size, (place, extent) in zip(at, inner, extents):
        position = digit + (place * size - RADIUS)
        valid = valid & (position >= 0) & (position < extent)
    row = lax.broadcasted_iota(jnp.int32, (size_z, 1), 0)
    for h in range(heads):
        turned = jnp.broadcast_to(base[h : h + 1], (size_z, lanes))
        bit = 1
        while bit < size_z:
            turned = jnp.where((row & bit) > 0, pltpu.roll(turned, bit, 1), turned)
            bit *= 2
        for x in range(size_x):
            for y in range(size_y):
                shift = (x * pad_y + y) * pad_z
                moved = pltpu.roll(turned, shift, 1) if shift else turned
                at_row = ((h * size_x + x) * size_y + y) * size_z
                table[at_row : at_row + size_z, :] = jnp.where(valid, moved, FAR)


def bias_fold(d_scores, inner, dims, lanes):
    size_x, size_y, size_z = inner
    _, pad_y, pad_z = dims
    total = None
    for x in range(size_x):
        for y in range(size_y):
            at_row = (x * size_y + y) * size_z
            shift = (x * pad_y + y) * pad_z
            part = d_scores[at_row : at_row + size_z, :]
            part = pltpu.roll(part, lanes - shift, 1) if shift else part
            total = part if total is None else total + part
    rows = size_z
    while rows > 8:
        rows //= 2
        total = total[:rows] + pltpu.roll(total[rows:], lanes - rows, 1)
    step = rows // 2
    while step >= 1:
        moved = pltpu.roll(total, lanes - step, 1)
        total = total + pltpu.roll(moved, rows - step, 0)
        step //= 2
    return total[0:1]


def normed(x, gain):
    inverse = lax.rsqrt(jnp.mean(x * x, axis=-1, keepdims=True) + 1e-06)
    scaled = x * inverse
    return (scaled * gain).astype(BF), scaled, inverse


def attention_grads(
    padded, local, gain, project_ref, output_ref, go, table, probs_s, low_s, inner, dims, heads
):
    lanes, channels = padded.shape
    rows = local.shape[0]
    head = channels // heads
    scale = head ** (-0.5)
    hidden, scaled, _ = normed(padded, gain)
    hidden_l, scaled_l, inverse_l = normed(local, gain)
    keys = jnp.dot(hidden, project_ref[:, channels : 2 * channels], preferred_element_type=F32).astype(BF)
    values = jnp.dot(hidden, project_ref[:, 2 * channels :], preferred_element_type=F32).astype(BF)
    queries = jnp.dot(hidden_l, project_ref[:, :channels], preferred_element_type=F32).astype(BF)
    d_att = dot(go, output_ref[...], (1, 1)).astype(BF)
    column = lax.broadcasted_iota(jnp.int32, (1, channels), 1)
    attended = jnp.zeros((rows, channels), F32)
    d_query = jnp.zeros((rows, channels), F32)
    query_parts, grad_parts, bias_parts = [], [], []
    for h in range(heads):
        mine = (column >= h * head) & (column < (h + 1) * head)
        q = jnp.where(mine, queries.astype(F32), 0.0).astype(BF)
        da = jnp.where(mine, d_att.astype(F32), 0.0).astype(BF)
        query_parts.append(q)
        grad_parts.append(da)
        span = slice(h * rows, (h + 1) * rows)
        scores = dot(q, keys, (1, 1)) * scale + table[span, :]
        weights = jnp.exp(scores - jnp.max(scores, axis=1, keepdims=True))
        probs = weights * (1.0 / jnp.sum(weights, axis=1, keepdims=True))
        probs_low = probs.astype(BF)
        probs_s[span, :] = probs_low
        gathered = jnp.dot(probs_low, values, preferred_element_type=F32)
        gathered = jnp.where(mine, gathered, 0.0).astype(BF).astype(F32)
        attended = attended + gathered
        centre = jnp.sum(da.astype(F32) * gathered, axis=1, keepdims=True)
        d_scores = probs * (dot(da, values, (1, 1)) - centre)
        bias_parts.append(bias_fold(d_scores, inner, dims, lanes))
        low = (d_scores * scale).astype(BF)
        low_s[span, :] = low
        d_query = d_query + jnp.where(mine, jnp.dot(low, keys, preferred_element_type=F32), 0.0)
    attended = attended.astype(BF)
    d_keys = dot(low_s[...], jnp.concatenate(query_parts, axis=0), (0, 0)).astype(BF)
    d_values = dot(probs_s[...], jnp.concatenate(grad_parts, axis=0), (0, 0)).astype(BF)
    d_query = d_query.astype(BF)
    d_hidden = dot(d_keys, project_ref[:, channels : 2 * channels], (1, 1)) + dot(
        d_values, project_ref[:, 2 * channels :], (1, 1)
    )
    d_hidden_l = dot(d_query, project_ref[:, :channels], (1, 1))
    project = (
        dot(hidden_l, d_query, (0, 0)),
        dot(hidden, d_keys, (0, 0)),
        dot(hidden, d_values, (0, 0)),
    )
    output = dot(attended, go, (0, 0))
    gain_sum = jnp.sum(d_hidden * scaled, axis=0, keepdims=True) + jnp.sum(
        d_hidden_l * scaled_l, axis=0, keepdims=True
    )
    folded = jnp.concatenate(bias_parts + [jnp.zeros((8 - heads, lanes), F32)], axis=0)
    bias_sum = lax.dot_general(
        folded,
        one_hot(dims, lanes),
        (((1,), (1,)), ((), ())),
        precision=lax.Precision.HIGHEST,
        preferred_element_type=F32,
    )
    return d_hidden, d_hidden_l, project, output, gain_sum, bias_sum, scaled_l, inverse_l


def kernel(
    inner, dims, sizes, padded_ref, local_ref, gain_ref, project_ref, output_ref, bias_ref, go_ref,
    dh_ref, dhl_ref, sums_ref, table, probs_s, low_s, spread,
):
    lanes, channels = padded_ref.shape
    extents = [
        (lax.axis_index(axis), size * cells)
        for axis, size, cells in zip(("gx", "gy", "gz"), sizes, inner)
    ]
    bias_table(bias_ref, spread, table, inner, dims, lanes, extents)
    d_hidden, d_hidden_l, project, output, gain_sum, bias_sum, _, _ = attention_grads(
        padded_ref[...], local_ref[...].astype(F32), gain_ref[...], project_ref, output_ref,
        go_ref[...], table, probs_s, low_s, inner, dims, bias_ref.shape[0],
    )
    dh_ref[...] = d_hidden
    dhl_ref[...] = d_hidden_l
    for i in range(3):
        sums_ref[i * channels : (i + 1) * channels, :] = project[i]
    sums_ref[3 * channels : 4 * channels, :] = output
    sums_ref[4 * channels : 4 * channels + 8, :] = bias_sum
    sums_ref[4 * channels + 8 : 4 * channels + 16, :] = jnp.broadcast_to(gain_sum, (8, channels))


def with_halo(array, sides, width):
    for axis, dim in sides:
        size, length = (lax.axis_size(axis), array.shape[dim])
        up = [(i, i + 1) for i in range(size - 1)]
        down = [(j, i) for i, j in up]
        last = lax.slice_in_dim(array, length - width, length, axis=dim)
        leading = lax.slice_in_dim(array, 0, width, axis=dim)
        before = lax.ppermute(last, axis, up)
        after = lax.ppermute(leading, axis, down)
        array = jnp.concatenate([before, array, after], axis=dim)
    return array


def fold_halo(array, sides, width):
    for axis, dim in sides:
        size, length = (lax.axis_size(axis), array.shape[dim])
        up = [(i, i + 1) for i in range(size - 1)]
        down = [(j, i) for i, j in up]
        low = lax.ppermute(lax.slice_in_dim(array, 0, width, axis=dim), axis, down)
        high = lax.ppermute(lax.slice_in_dim(array, length - width, length, axis=dim), axis, up)
        array = lax.slice_in_dim(array, width, length - width, axis=dim)
        inner = length - 2 * width
        pads = [[(0, 0)] * array.ndim for _ in range(2)]
        pads[0][dim] = (inner - width, 0)
        pads[1][dim] = (0, inner - width)
        array = array + jnp.pad(low, pads[0]) + jnp.pad(high, pads[1])
    return array


def shards(tokens, norm_gain, project_weight, output_weight, position_bias, grad_output):
    inner, channels = tokens.shape[:3], tokens.shape[3]
    heads = position_bias.shape[0]
    sizes = tuple(lax.axis_size(axis) for axis in ("gx", "gy", "gz"))
    dims = tuple(size + 2 * RADIUS for size in inner)
    rows = inner[0] * inner[1] * inner[2]
    count = dims[0] * dims[1] * dims[2]
    lanes = -(-count // 128) * 128
    factor = (rows * sizes[0] * sizes[1] * sizes[2]) ** (-0.5)
    padded = with_halo(tokens, (("gx", 0), ("gy", 1), ("gz", 2)), RADIUS)
    padded = jnp.pad(padded.astype(F32).reshape(count, channels), ((0, lanes - count), (0, 0)))
    d_hidden, d_hidden_l, sums = pl.pallas_call(
        functools.partial(kernel, inner, dims, sizes),
        out_shape=(
            jax.ShapeDtypeStruct((lanes, channels), F32),
            jax.ShapeDtypeStruct((rows, channels), F32),
            jax.ShapeDtypeStruct((4 * channels + 16, channels), F32),
        ),
        in_specs=[pl.BlockSpec(memory_space=pltpu.VMEM)] * 7,
        out_specs=(pl.BlockSpec(memory_space=pltpu.VMEM),) * 3,
        scratch_shapes=[
            pltpu.VMEM((heads * rows, lanes), F32),
            pltpu.VMEM((heads * rows, lanes), BF),
            pltpu.VMEM((heads * rows, lanes), BF),
            pltpu.VMEM((8, 128), F32),
        ],
        compiler_params=pltpu.CompilerParams(vmem_limit_bytes=40 * 2**20),
    )(
        padded,
        tokens.reshape(rows, channels),
        norm_gain.reshape(1, channels),
        project_weight,
        output_weight,
        position_bias,
        grad_output.reshape(rows, channels),
    )
    summed = lax.psum(sums, ("gx", "gy", "gz")) * factor
    grid = d_hidden[:count].reshape(dims + (channels,))
    mine = fold_halo(grid, (("gz", 2), ("gy", 1), ("gx", 0)), RADIUS).reshape(rows, channels)
    d_scaled = (mine + d_hidden_l) * norm_gain
    x = tokens.reshape(rows, channels).astype(F32)
    inverse = lax.rsqrt(jnp.mean(x * x, axis=-1, keepdims=True) + 1e-06)
    scaled = x * inverse
    token_grad = inverse * (d_scaled - scaled * jnp.mean(d_scaled * scaled, axis=-1, keepdims=True))
    project_grad = jnp.concatenate(
        [summed[i * channels : (i + 1) * channels] for i in range(3)], axis=1
    )
    return (
        token_grad.reshape(tokens.shape),
        project_grad,
        summed[3 * channels : 4 * channels],
        summed[4 * channels + 8],
        summed[4 * channels : 4 * channels + heads, : WIN**3],
    )


def solution(mesh):
    tokens = P(("groups", "gx"), "gy", "gz", None)
    return jax.shard_map(
        shards,
        mesh=mesh,
        in_specs=(tokens, P(), P(), P(), P(), tokens),
        out_specs=(tokens, P("groups", None), P("groups", None), P("groups"), P("groups", None)),
        check_vma=False,
    )
```

time: 319 us -> 153 us (0.48)
  local copies, waits for them, and re-layouts: 105 us -> 2.87 us
  other arithmetic: 39.5 us -> 3.05 us
  waiting for transfers between devices: 121 us -> 94.7 us
  loops' own time: 8.87 us -> 0 us
  Pallas kernels: 0 us -> 7.19 us
  starting transfers between devices: 26.3 us -> 30.3 us
    another operation x477 -> x0, local copies, waits for them, and re-layouts: 41.1 us -> none  [the longest x475 41 us: window_stack(): jnp.stack([part[:, :, shift:shift + size_z] for shift in range(WIN)])]
    while x401 -> x0, local copies, waits for them, and re-layouts: 25.8 us -> none
    slice x231 -> x6, local copies, waits for them, and re-layouts: 25.4 us -> 1.32 us  [the longest x1 0.65 us: shards(): summed[3 * channels:4 * channels]]
    transpose x75 -> x0, other arithmetic: 17.7 us -> none  [expand_heads(): return jnp.repeat(jnp.swapaxes(values, 1, 2), head_size, axis=2)]
    ppermute x0 -> x6, starting transfers between devices: none -> 16.8 us  [the longest x3 12.9 us: fold_halo(): lax.ppermute(lax.slice_in_dim(array, length - width, length, axis=dim), a...]
    ppermute x6 -> x3, waiting for transfers between devices: 17.4 us -> 1.03 us  [with_halo(): before = lax.ppermute(last, axis, up)]
    ppermute x6 -> x3, starting transfers between devices: 18.5 us -> 9.62 us  [with_halo(): before = lax.ppermute(last, axis, up)]
    another operation x3 -> x0, loops' own time: 8.87 us -> none  [the longest x1 3.57 us: attend_block(): lax.fori_loop(first_turn, last_turn, back_turn, start_back)]
  transfers between devices with their start and end apart: 13 -> 13, of which waited for: 10 -> 8; matrix products, arithmetic and copies ran while one was open for 1% -> 2% of each run, Pallas kernels for 0% -> 0%
where the time goes in v1:
time: 153 us; the launch traced here: 152 us
  waiting for transfers between devices  94.7 us (62%)
  starting transfers between devices  30.3 us (20%)
  between operations  14.3 us (9%)
  Pallas kernels  7.19 us (5%)
  other arithmetic  3.05 us (2%)
  local copies, waits for them, and re-layouts  2.87 us (2%)
    psum x1, waiting for transfers between devices, shards(): summed = lax.psum(sums, ('gx', 'gy', 'gz')) * factor  81.7 us
    ppermute x3, starting transfers between devices, fold_halo(): lax.ppermute(lax.slice_in_dim(array, length - width, length, axis=dim), a...  12.9 us
    ppermute x3, waiting for transfers between devices, with_halo(): after = lax.ppermute(leading, axis, down)  10 us
    ppermute x3, starting transfers between devices, with_halo(): before = lax.ppermute(last, axis, up)  9.62 us
    pallas_call x1, Pallas kernels, shards(): pl.pallas_call(functools.partial(kernel, inner, dims, sizes), out_shape=(...  7.19 us
    ppermute x3, starting transfers between devices, fold_halo(): low = lax.ppermute(lax.slice_in_dim(array, 0, width, axis=dim), axis, down)  3.88 us
    ppermute x3, starting transfers between devices, with_halo(): after = lax.ppermute(leading, axis, down)  3.88 us
  transfers between devices with their start and end apart: 13, of which 8 were waited for; matrix products, arithmetic and copies ran while one was open for 2% of the time, Pallas kernels for 0%

profile of v1, /device:TPU:0, one launch (start us, length us, event | category | flops | bytes accessed | tf_op | source)
XLA Modules:
  0.0 152.4 jit_solution(9634426592851381893)
XLA Ops:
  7.2 4.9 %collective-permute-start = (bf16[2,4,16,128]{3,2,1,0:T(8,128)(2,1)}, bf16[2,4,16,128]{3,2,1,0:T(8,128)(2,1)S(1)}, u32[]{:S(2)}, u32[]{:S(2)}) collective-permute-start(bf16[2,4,16,128]{3,2,1,0:T(8,128)(2,1)} %param.6), channel_id=1, source_target_pairs={{0,4},{4,8},{8,12},{1,5},{5,9},{9,13},{2,6},{6,10},{10,14},{3,7},{... | collective-permute-start | bytes 98312 | tf_op jit(solution)/shard_map/ppermute | solution.py:201
  12.2 1.3 collective-permute-start.1
  14.1 4.1 %collective-permute-done.1 = bf16[2,4,16,128]{3,2,1,0:T(8,128)(2,1)S(1)} collective-permute-done((bf16[2,4,16,128]{3,2,1,0:T(8,128)(2,1)}, bf16[2,4,16,128]{3,2,1,0:T(8,128)(2,1)S(1)}, u32[]{:S(2)}, u32[]{:S(2)}) %collective-permute-start.1) | collective-permute-done | bytes 32800 | tf_op jit(solution)/shard_map/ppermute | solution.py:202
  18.2 3.4 %collective-permute-start.2 = (bf16[6,2,16,128]{3,2,1,0:T(8,128)(2,1)S(1)}, bf16[6,2,16,128]{3,2,1,0:T(8,128)(2,1)S(1)}, u32[]{:S(2)}, u32[]{:S(2)}) collective-permute-start(bf16[6,2,16,128]{3,2,1,0:T(8,128)(2,1)S(1)} %get-tuple-element.23), channel_id=1, source_target_pairs={{0,2},{1,3},{4,6},{5,7},{8,10},{9,11},{12,14},{13,15},{16,18},{17,... | collective-permute-start | bytes 147464 | tf_op jit(solution)/shard_map/ppermute | solution.py:201
  21.6 1.3 collective-permute-start.3
  23.3 4.3 %collective-permute-done.3 = bf16[6,2,16,128]{3,2,1,0:T(8,128)(2,1)S(1)} collective-permute-done((bf16[6,2,16,128]{3,2,1,0:T(8,128)(2,1)S(1)}, bf16[6,2,16,128]{3,2,1,0:T(8,128)(2,1)S(1)}, u32[]{:S(2)}, u32[]{:S(2)}) %collective-permute-start.3) | collective-permute-done | bytes 49184 | tf_op jit(solution)/shard_map/ppermute | solution.py:202
  27.6 1.3 collective-permute-start.4
  28.9 1.3 collective-permute-start.5
  30.3 1.7 %collective-permute-done.5 = bf16[6,8,2,128]{3,2,1,0:T(2,128)(2,1)S(1)} collective-permute-done((bf16[6,8,2,128]{3,2,1,0:T(2,128)(2,1)S(1)}, bf16[6,8,2,128]{3,2,1,0:T(2,128)(2,1)S(1)}, u32[]{:S(2)}, u32[]{:S(2)}) %collective-permute-start.5) | collective-permute-done | bytes 24608 | tf_op jit(solution)/shard_map/ppermute | solution.py:202
  32.4 0.8 copy-done.1
  33.2 7.2 %shard_map.101 = (f32[1024,128]{1,0:T(8,128)S(1)}, f32[128,128]{1,0:T(8,128)S(1)}, f32[528,128]{1,0:T(8,128)}) custom-call(f32[1024,128]{1,0:T(8,128)S(1)} %pad_convert_fusion.padded_ref, bf16[128,128]{1,0:T(8,128)(2,1)S(1)} %bitcast.16, f32[1,128]{1,0:T(1,128)S(1)} %bitcast.18, bf16[128,384]{1,0:T(8,128)(2,1)S(1)} %copy-done.1, ...), custom_call_target="tpu_custom_call" | custom-call | tf_op jit(solution)/shard_map/pallas_call | solution.py:234
  40.5 1.3 collective-permute-start.6
  41.8 3.0 %collective-permute-start.7 = (f32[6,8,2,128]{3,2,1,0:T(2,128)S(1)}, f32[6,8,2,128]{3,2,1,0:T(2,128)S(1)}, u32[]{:S(2)}, u32[]{:S(2)}) collective-permute-start(f32[6,8,2,128]{3,2,1,0:T(2,128)S(1)} %get-tuple-element.12), channel_id=1, source_target_pairs={{0,1},{2,3},{4,5},{6,7},{8,9},{10,11},{12,13},{14,15},{16,17},{18,... | collective-permute-start | bytes 147464 | tf_op jit(solution)/shard_map/ppermute | solution.py:213
  45.0 0.7 collective-permute-done.7
  45.8 1.3 collective-permute-start.8
  47.1 4.6 %collective-permute-start.9 = (f32[6,2,16,128]{3,2,1,0:T(8,128)S(1)}, f32[6,2,16,128]{3,2,1,0:T(8,128)S(1)}, u32[]{:S(2)}, u32[]{:S(2)}) collective-permute-start(f32[6,2,16,128]{3,2,1,0:T(8,128)S(1)} %get-tuple-element.14), channel_id=1, source_target_pairs={{0,2},{1,3},{4,6},{5,7},{8,10},{9,11},{12,14},{13,15},{16,18},{17,... | collective-permute-start | bytes 294920 | tf_op jit(solution)/shard_map/ppermute | solution.py:213
  51.6 81.7 %all-reduce.7.cloned.1.call-done = f32[528,128]{1,0:T(8,128)} async-done(((f32[528,128]{1,0:T(8,128)}), f32[528,128]{1,0:T(8,128)}) %all-reduce.7.cloned.1.call-update) | async-done | bytes 270352 | tf_op jit(solution)/shard_map/psum | solution.py:259
  133.3 1.0 broadcast_multiply_fusion
  134.3 0.6 fusion.6
  136.1 1.3 collective-permute-start.10
  137.4 5.3 %collective-permute-start.11 = (f32[2,4,16,128]{3,2,1,0:T(8,128)S(1)}, f32[2,4,16,128]{3,2,1,0:T(8,128)S(1)}, u32[]{:S(2)}, u32[]{:S(2)}) collective-permute-start(f32[2,4,16,128]{3,2,1,0:T(8,128)S(1)} %get-tuple-element.20), channel_id=1, source_target_pairs={{0,4},{4,8},{8,12},{1,5},{5,9},{9,13},{2,6},{6,10},{10,14},{3,7},{... | collective-permute-start | bytes 196616 | tf_op jit(solution)/shard_map/ppermute | solution.py:213
  142.7 0.7 pad_maximum_fusion.1
  143.4 1.2 collective-permute-done.11
  144.8 0.7 subtract_multiply_fusion
  (43 shorter events, 3.2 us)
Async XLA Ops:
  7.2 6.9 %copy-start = (bf16[2,4,16,128]{3,2,1,0:T(8,128)(2,1)S(1)}, bf16[2,4,16,128]{3,2,1,0:T(8,128)(2,1)}, u32[]{:S(2)}) copy-start(bf16[2,4,16,128]{3,2,1,0:T(8,128)(2,1)} %param.6) | copy-start | bytes 98308
  7.2 126.1 %all-reduce.7.cloned.1.call-start = ((), (), s32[]{:S(2)}) async-start(), calls=%async_computation | async-start | bytes 540672 | tf_op jit(solution)/shard_map/psum | solution.py:259
  7.2 6.8 %collective-permute-start = (bf16[2,4,16,128]{3,2,1,0:T(8,128)(2,1)}, bf16[2,4,16,128]{3,2,1,0:T(8,128)(2,1)S(1)}, u32[]{:S(2)}, u32[]{:S(2)}) collective-permute-start(bf16[2,4,16,128]{3,2,1,0:T(8,128)(2,1)} %param.6), channel_id=1, source_target_pairs={{0,4},{4,8},{8,12},{1,5},{5,9},{9,13},{2,6},{6,10},{10,14},{3,7},{... | collective-permute-start | bytes 98312 | tf_op jit(solution)/shard_map/ppermute | solution.py:201
  12.2 6.0 %collective-permute-start.1 = (bf16[2,4,16,128]{3,2,1,0:T(8,128)(2,1)}, bf16[2,4,16,128]{3,2,1,0:T(8,128)(2,1)S(1)}, u32[]{:S(2)}, u32[]{:S(2)}) collective-permute-start(bf16[2,4,16,128]{3,2,1,0:T(8,128)(2,1)} %param.6), channel_id=1, source_target_pairs={{4,0},{8,4},{12,8},{5,1},{9,5},{13,9},{6,2},{10,6},{14,10},{7,3},{... | collective-permute-start | bytes 98312 | tf_op jit(solution)/shard_map/ppermute | solution.py:202
  18.2 5.1 %collective-permute-start.2 = (bf16[6,2,16,128]{3,2,1,0:T(8,128)(2,1)S(1)}, bf16[6,2,16,128]{3,2,1,0:T(8,128)(2,1)S(1)}, u32[]{:S(2)}, u32[]{:S(2)}) collective-permute-start(bf16[6,2,16,128]{3,2,1,0:T(8,128)(2,1)S(1)} %get-tuple-element.23), channel_id=1, source_target_pairs={{0,2},{1,3},{4,6},{5,7},{8,10},{9,11},{12,14},{13,15},{16,18},{17,... | collective-permute-start | bytes 147464 | tf_op jit(solution)/shard_map/ppermute | solution.py:201
  21.6 6.0 %collective-permute-start.3 = (bf16[6,2,16,128]{3,2,1,0:T(8,128)(2,1)S(1)}, bf16[6,2,16,128]{3,2,1,0:T(8,128)(2,1)S(1)}, u32[]{:S(2)}, u32[]{:S(2)}) collective-permute-start(bf16[6,2,16,128]{3,2,1,0:T(8,128)(2,1)S(1)} %get-tuple-element.24), channel_id=1, source_target_pairs={{2,0},{3,1},{6,4},{7,5},{10,8},{11,9},{14,12},{15,13},{18,16},{19,... | collective-permute-start | bytes 147464 | tf_op jit(solution)/shard_map/ppermute | solution.py:202
  27.6 2.7 %collective-permute-start.4 = (bf16[6,8,2,128]{3,2,1,0:T(2,128)(2,1)S(1)}, bf16[6,8,2,128]{3,2,1,0:T(2,128)(2,1)S(1)}, u32[]{:S(2)}, u32[]{:S(2)}) collective-permute-start(bf16[6,8,2,128]{3,2,1,0:T(2,128)(2,1)S(1)} %get-tuple-element.21), channel_id=1, source_target_pairs={{0,1},{2,3},{4,5},{6,7},{8,9},{10,11},{12,13},{14,15},{16,17},{18,... | collective-permute-start | bytes 73736 | tf_op jit(solution)/shard_map/ppermute | solution.py:201
  28.9 3.1 %collective-permute-start.5 = (bf16[6,8,2,128]{3,2,1,0:T(2,128)(2,1)S(1)}, bf16[6,8,2,128]{3,2,1,0:T(2,128)(2,1)S(1)}, u32[]{:S(2)}, u32[]{:S(2)}) collective-permute-start(bf16[6,8,2,128]{3,2,1,0:T(2,128)(2,1)S(1)} %get-tuple-element.22), channel_id=1, source_target_pairs={{1,0},{3,2},{5,4},{7,6},{9,8},{11,10},{13,12},{15,14},{17,16},{19,... | collective-permute-start | bytes 73736 | tf_op jit(solution)/shard_map/ppermute | solution.py:202
  32.2 0.9 copy-start.1
  32.3 0.9 copy-start.2
  32.3 0.9 copy-start.3
  32.3 0.8 copy-start.5
  32.3 0.8 copy-start.4
  40.5 4.5 %collective-permute-start.6 = (f32[6,8,2,128]{3,2,1,0:T(2,128)S(1)}, f32[6,8,2,128]{3,2,1,0:T(2,128)S(1)}, u32[]{:S(2)}, u32[]{:S(2)}) collective-permute-start(f32[6,8,2,128]{3,2,1,0:T(2,128)S(1)} %get-tuple-element.11), channel_id=1, source_target_pairs={{1,0},{3,2},{5,4},{7,6},{9,8},{11,10},{13,12},{15,14},{17,16},{19,... | collective-permute-start | bytes 147464 | tf_op jit(solution)/shard_map/ppermute | solution.py:212
  41.8 3.9 %collective-permute-start.7 = (f32[6,8,2,128]{3,2,1,0:T(2,128)S(1)}, f32[6,8,2,128]{3,2,1,0:T(2,128)S(1)}, u32[]{:S(2)}, u32[]{:S(2)}) collective-permute-start(f32[6,8,2,128]{3,2,1,0:T(2,128)S(1)} %get-tuple-element.12), channel_id=1, source_target_pairs={{0,1},{2,3},{4,5},{6,7},{8,9},{10,11},{12,13},{14,15},{16,17},{18,... | collective-permute-start | bytes 147464 | tf_op jit(solution)/shard_map/ppermute | solution.py:213
  45.8 90.3 %collective-permute-start.8 = (f32[6,2,16,128]{3,2,1,0:T(8,128)S(1)}, f32[6,2,16,128]{3,2,1,0:T(8,128)S(1)}, u32[]{:S(2)}, u32[]{:S(2)}) collective-permute-start(f32[6,2,16,128]{3,2,1,0:T(8,128)S(1)} %get-tuple-element.13), channel_id=1, source_target_pairs={{2,0},{3,1},{6,4},{7,5},{10,8},{11,9},{14,12},{15,13},{18,16},{19,... | collective-permute-start | bytes 294920 | tf_op jit(solution)/shard_map/ppermute | solution.py:212
  47.1 89.0 %collective-permute-start.9 = (f32[6,2,16,128]{3,2,1,0:T(8,128)S(1)}, f32[6,2,16,128]{3,2,1,0:T(8,128)S(1)}, u32[]{:S(2)}, u32[]{:S(2)}) collective-permute-start(f32[6,2,16,128]{3,2,1,0:T(8,128)S(1)} %get-tuple-element.14), channel_id=1, source_target_pairs={{0,2},{1,3},{4,6},{5,7},{8,10},{9,11},{12,14},{13,15},{16,18},{17,... | collective-permute-start | bytes 294920 | tf_op jit(solution)/shard_map/ppermute | solution.py:213
  136.1 7.3 %collective-permute-start.10 = (f32[2,4,16,128]{3,2,1,0:T(8,128)S(1)}, f32[2,4,16,128]{3,2,1,0:T(8,128)S(1)}, u32[]{:S(2)}, u32[]{:S(2)}) collective-permute-start(f32[2,4,16,128]{3,2,1,0:T(8,128)S(1)} %get-tuple-element.19), channel_id=1, source_target_pairs={{4,0},{8,4},{12,8},{5,1},{9,5},{13,9},{6,2},{10,6},{14,10},{7,3},{... | collective-permute-start | bytes 196616 | tf_op jit(solution)/shard_map/ppermute | solution.py:212
  137.4 7.2 %collective-permute-start.11 = (f32[2,4,16,128]{3,2,1,0:T(8,128)S(1)}, f32[2,4,16,128]{3,2,1,0:T(8,128)S(1)}, u32[]{:S(2)}, u32[]{:S(2)}) collective-permute-start(f32[2,4,16,128]{3,2,1,0:T(8,128)S(1)} %get-tuple-element.20), channel_id=1, source_target_pairs={{0,4},{4,8},{8,12},{1,5},{5,9},{9,13},{2,6},{6,10},{10,14},{3,7},{... | collective-permute-start | bytes 196616 | tf_op jit(solution)/shard_map/ppermute | solution.py:213
Sparse Core Ops, SparseCore 0:
  45.1 88.2 all-reduce.6

commit v2 on v1

--- a/solution.py
+++ b/solution.py
@@ -103,7 +103,7 @@
 
 
 def attention_grads(
-    padded, local, gain, project_ref, output_ref, go, table, probs_s, low_s, inner, dims, heads
+    padded, local, gain, project_ref, output_ref, go, table, probs_s, low_s, inner, dims, heads, send_hidden
 ):
     lanes, channels = padded.shape
     rows = local.shape[0]
@@ -147,6 +147,7 @@
     d_hidden = dot(d_keys, project_ref[:, channels : 2 * channels], (1, 1)) + dot(
         d_values, project_ref[:, 2 * channels :], (1, 1)
     )
+    send_hidden(d_hidden)
     d_hidden_l = dot(d_query, project_ref[:, :channels], (1, 1))
     project = (
         dot(hidden_l, d_query, (0, 0)),
@@ -168,112 +169,302 @@
     return d_hidden, d_hidden_l, project, output, gain_sum, bias_sum, scaled_l, inverse_l
 
 
+MESH = pl.DeviceIdType.MESH
+AXES = ("gx", "gy", "gz")
+TURNS = [(x, y, z) for x in (0, -1, 1) for y in (0, -1, 1) for z in (0, -1, 1)][1:]
+FLAT = [turn for turn in TURNS if turn[2] == 0]
+EDGES = [turn for turn in TURNS if turn[2] != 0]
+
+
+def span_of(turn, size):
+    return {0: (0, size), 1: (size - RADIUS, size), -1: (0, RADIUS)}[turn]
+
+
+def rim_of(turn, size):
+    return {
+        0: (RADIUS, size + RADIUS),
+        1: (size + RADIUS, size + 2 * RADIUS),
+        -1: (0, RADIUS),
+    }[turn]
+
+
 def kernel(
-    inner, dims, sizes, padded_ref, local_ref, gain_ref, project_ref, output_ref, bias_ref, go_ref,
-    dh_ref, dhl_ref, sums_ref, table, probs_s, low_s, spread,
+    inner, dims, sizes, factor, chunk,
+    tokens_ref, gain_ref, project_ref, output_ref, bias_ref, go_ref,
+    token_out, project_out, output_out, gain_out, bias_out,
+    table, probs_s, low_s, spread,
+    edge_f, edge, main, rims, padded, hidden_f, pack_f, out_main, out_edge, in_main, in_edge,
+    sums_f, sums, parts, final,
+    tok_send, tok_recv, ret_send, ret_recv, rs_send, rs_recv, ag_send, ag_recv,
 ):
-    lanes, channels = padded_ref.shape
-    extents = [
-        (lax.axis_index(axis), size * cells)
-        for axis, size, cells in zip(("gx", "gy", "gz"), sizes, inner)
+    size_x, size_y, size_z = inner
+    pad_x, pad_y, pad_z = dims
+    rows = size_x * size_y * size_z
+    lanes, channels = padded.shape
+    heads = bias_ref.shape[0]
+    here = [lax.axis_index(axis) for axis in AXES]
+    count = sizes[0] * sizes[1] * sizes[2]
+    me = (here[0] * sizes[1] + here[1]) * sizes[2] + here[2]
+
+    def peer(k):
+        other = lax.rem(me + k, count)
+        rest = lax.div(other, sizes[2])
+        place = (lax.div(rest, sizes[1]), lax.rem(rest, sizes[1]), lax.rem(other, sizes[2]))
+        return other, dict(zip(AXES, place))
+
+    def exists(turn, sign):
+        ok = None
+        for at, size, step in zip(here, sizes, turn):
+            if step:
+                this = (at + sign * step >= 0) & (at + sign * step < size)
+                ok = this if ok is None else ok & this
+        return ok
+
+    def neighbour(turn):
+        return {axis: at + step for axis, at, step in zip(AXES, here, turn)}
+
+    main[...] = jnp.zeros_like(main)
+    rims[...] = jnp.zeros_like(rims)
+    in_main[...] = jnp.zeros_like(in_main)
+    in_edge[...] = jnp.zeros_like(in_edge)
+    barrier = pltpu.get_barrier_semaphore()
+
+    def greet(k, carry):
+        pl.semaphore_signal(barrier, inc=1, device_id=peer(k)[1], device_id_type=MESH)
+        return carry
+
+    lax.fori_loop(1, count, greet, 0)
+    for x in range(size_x):
+        for y in range(size_y):
+            line = tokens_ref[x, y].astype(F32)
+            at = (x * size_y + y) * RADIUS
+            edge_f[0, at : at + RADIUS, :] = line[:RADIUS]
+            edge_f[1, at : at + RADIUS, :] = line[size_z - RADIUS :]
+    edge[...] = edge_f[...].astype(BF)
+    pl.semaphore_wait(barrier, count - 1)
+
+    def token_copy(turn):
+        n = TURNS.index(turn)
+        if turn[2]:
+            source = edge.at[1 if turn[2] > 0 else 0]
+            target = rims.at[EDGES.index(turn)]
+        else:
+            (x0, x1), (y0, y1) = (span_of(t, s) for t, s in zip(turn[:2], inner[:2]))
+            (u0, u1), (v0, v1) = (rim_of(-t, s) for t, s in zip(turn[:2], inner[:2]))
+            source = tokens_ref.at[x0:x1, y0:y1]
+            target = main.at[u0:u1, v0:v1]
+        return pltpu.make_async_remote_copy(
+            src_ref=source, dst_ref=target, send_sem=tok_send.at[n], recv_sem=tok_recv.at[n],
+            device_id=neighbour(turn), device_id_type=MESH,
+        )
+
+    def grad_copy(turn):
+        n = TURNS.index(turn)
+        if turn[2]:
+            source, target = (buffer.at[EDGES.index(turn)] for buffer in (out_edge, in_edge))
+        else:
+            (u0, u1), (v0, v1) = (rim_of(t, s) for t, s in zip(turn[:2], inner[:2]))
+            source = out_main.at[u0:u1, v0:v1]
+            target = in_main.at[FLAT.index(turn), 0 : u1 - u0, 0 : v1 - v0]
+        return pltpu.make_async_remote_copy(
+            src_ref=source, dst_ref=target, send_sem=ret_send.at[n], recv_sem=ret_recv.at[n],
+            device_id=neighbour(turn), device_id_type=MESH,
+        )
+
+    def every(make, sign, what):
+        for turn in TURNS:
+            pl.when(exists(turn, sign))(lambda turn=turn: getattr(make(turn), what)())
+
+    every(token_copy, 1, "start")
+    bias_table(
+        bias_ref, spread, table, inner, dims, lanes,
+        [(at, size * cells) for at, size, cells in zip(here, sizes, inner)],
+    )
+    every(token_copy, -1, "wait_recv")
+
+    filled = pad_x * pad_y * pad_z
+    if filled < lanes:
+        padded[filled:, :] = jnp.zeros((lanes - filled, channels), F32)
+    sides = [
+        [(t, u - rim_of(-t, s)[0] + span_of(t, s)[0]) for u in range(s + 2 * RADIUS)
+         for t in (0, 1, -1) if rim_of(-t, s)[0] <= u < rim_of(-t, s)[1]]
+        for s in inner[:2]
     ]
-    bias_table(bias_ref, spread, table, inner, dims, lanes, extents)
-    d_hidden, d_hidden_l, project, output, gain_sum, bias_sum, _, _ = attention_grads(
-        padded_ref[...], local_ref[...].astype(F32), gain_ref[...], project_ref, output_ref,
-        go_ref[...], table, probs_s, low_s, inner, dims, bias_ref.shape[0],
-    )
-    dh_ref[...] = d_hidden
-    dhl_ref[...] = d_hidden_l
+    for u in range(pad_x):
+        for v in range(pad_y):
+            (turn_x, x), (turn_y, y) = sides[0][u], sides[1][v]
+            at = (u * pad_y + v) * pad_z
+            own = turn_x == 0 and turn_y == 0
+            line = tokens_ref[x, y] if own else main[u, v]
+            padded[at + RADIUS : at + RADIUS + size_z, :] = line.astype(F32)
+            row = (x * size_y + y) * RADIUS
+            for turn_z, to in ((1, at), (-1, at + RADIUS + size_z)):
+                tile = rims[EDGES.index((turn_x, turn_y, turn_z))].astype(F32)
+                padded[to : to + RADIUS, :] = tile[row : row + RADIUS]
+
+    def send_hidden(d_hidden):
+        hidden_f[...] = d_hidden
+        pack_f[...] = jnp.zeros_like(pack_f)
+        for u in range(pad_x):
+            for v in range(pad_y):
+                (turn_x, x), (turn_y, y) = sides[0][u], sides[1][v]
+                at = (u * pad_y + v) * pad_z
+                out_main[u, v] = hidden_f[at + RADIUS : at + RADIUS + size_z, :].astype(BF)
+                row = (x * size_y + y) * RADIUS
+                for turn_z, to in ((-1, at), (1, at + RADIUS + size_z)):
+                    slot = EDGES.index((-turn_x, -turn_y, turn_z))
+                    pack_f[slot, row : row + RADIUS, :] = hidden_f[to : to + RADIUS, :]
+        out_edge[...] = pack_f[...].astype(BF)
+        every(grad_copy, 1, "start")
+
+    _, d_hidden_l, project, output, gain_sum, bias_sum, scaled, inverse = attention_grads(
+        padded[...], tokens_ref[...].astype(F32).reshape(rows, channels), gain_ref[...],
+        project_ref, output_ref, go_ref[...], table, probs_s, low_s, inner, dims, heads,
+        send_hidden,
+    )
+    used = 4 * channels
     for i in range(3):
-        sums_ref[i * channels : (i + 1) * channels, :] = project[i]
-    sums_ref[3 * channels : 4 * channels, :] = output
-    sums_ref[4 * channels : 4 * channels + 8, :] = bias_sum
-    sums_ref[4 * channels + 8 : 4 * channels + 16, :] = jnp.broadcast_to(gain_sum, (8, channels))
-
-
-def with_halo(array, sides, width):
-    for axis, dim in sides:
-        size, length = (lax.axis_size(axis), array.shape[dim])
-        up = [(i, i + 1) for i in range(size - 1)]
-        down = [(j, i) for i, j in up]
-        last = lax.slice_in_dim(array, length - width, length, axis=dim)
-        leading = lax.slice_in_dim(array, 0, width, axis=dim)
-        before = lax.ppermute(last, axis, up)
-        after = lax.ppermute(leading, axis, down)
-        array = jnp.concatenate([before, array, after], axis=dim)
-    return array
-
-
-def fold_halo(array, sides, width):
-    for axis, dim in sides:
-        size, length = (lax.axis_size(axis), array.shape[dim])
-        up = [(i, i + 1) for i in range(size - 1)]
-        down = [(j, i) for i, j in up]
-        low = lax.ppermute(lax.slice_in_dim(array, 0, width, axis=dim), axis, down)
-        high = lax.ppermute(lax.slice_in_dim(array, length - width, length, axis=dim), axis, up)
-        array = lax.slice_in_dim(array, width, length - width, axis=dim)
-        inner = length - 2 * width
-        pads = [[(0, 0)] * array.ndim for _ in range(2)]
-        pads[0][dim] = (inner - width, 0)
-        pads[1][dim] = (0, inner - width)
-        array = array + jnp.pad(low, pads[0]) + jnp.pad(high, pads[1])
-    return array
+        sums_f[i * channels : (i + 1) * channels, :] = project[i]
+    sums_f[3 * channels : used, :] = output
+    sums_f[used : used + 8, :] = bias_sum
+    sums_f[used + 8 : used + 16, :] = jnp.broadcast_to(gain_sum, (8, channels))
+    if count * chunk > used + 16:
+        sums_f[used + 16 :, :] = jnp.zeros((count * chunk - used - 16, channels), F32)
+    sums[...] = sums_f[...].astype(BF).reshape(count, chunk, channels)
+
+    def part_copy(k):
+        other, place = peer(k)
+        return pltpu.make_async_remote_copy(
+            src_ref=sums.at[other], dst_ref=parts.at[k], send_sem=rs_send.at[k],
+            recv_sem=rs_recv.at[k], device_id=place, device_id_type=MESH,
+        )
+
+    def whole_copy(k):
+        place = peer(k)[1]
+        return pltpu.make_async_remote_copy(
+            src_ref=final.at[me], dst_ref=final.at[me], send_sem=ag_send.at[k],
+            recv_sem=ag_recv.at[k], device_id=place, device_id_type=MESH,
+        )
+
+    def whole_arrival(k):
+        other = lax.rem(me + count - k, count)
+        return pltpu.make_async_remote_copy(
+            src_ref=final.at[other], dst_ref=final.at[other], send_sem=ag_send.at[k],
+            recv_sem=ag_recv.at[k], device_id=peer(k)[1], device_id_type=MESH,
+        )
+
+    def loop(body):
+        lax.fori_loop(1, count, lambda k, carry: (body(k), carry)[1], 0)
+
+    loop(lambda k: part_copy(k).start())
+
+    every(grad_copy, -1, "wait_recv")
+    norm_scaled = d_hidden_l
+    low = jnp.zeros(in_edge.shape[1:], F32)
+    high = jnp.zeros(in_edge.shape[1:], F32)
+    for n, turn in enumerate(EDGES):
+        if turn[2] > 0:
+            low = low + in_edge[n].astype(F32)
+        else:
+            high = high + in_edge[n].astype(F32)
+    for x in range(size_x):
+        for y in range(size_y):
+            at = ((x + RADIUS) * pad_y + y + RADIUS) * pad_z + RADIUS
+            line = hidden_f[at : at + size_z, :]
+            for n, (turn_x, turn_y, _) in enumerate(FLAT):
+                (x0, x1), (y0, y1) = span_of(-turn_x, size_x), span_of(-turn_y, size_y)
+                if x0 <= x < x1 and y0 <= y < y1:
+                    line = line + in_main[n, x - x0, y - y0].astype(F32)
+            to = (x * size_y + y) * size_z
+            row = (x * size_y + y) * RADIUS
+            padded[to : to + size_z, :] = line
+            padded[to : to + RADIUS, :] += low[row : row + RADIUS]
+            padded[to + size_z - RADIUS : to + size_z, :] += high[row : row + RADIUS]
+    d_scaled = (padded[0:rows, :] + norm_scaled) * gain_ref[...]
+    token_grad = inverse * (
+        d_scaled - scaled * jnp.mean(d_scaled * scaled, axis=-1, keepdims=True)
+    )
+    token_out[...] = token_grad.reshape(inner + (channels,))
+
+    loop(lambda k: part_copy(k).wait_recv())
+    total = lax.fori_loop(
+        1, count, lambda k, carry: carry + parts[k].astype(F32), sums[me].astype(F32)
+    )
+    final[me] = (total * factor).astype(BF)
+    loop(lambda k: whole_copy(k).start())
+    loop(lambda k: whole_arrival(k).wait_recv())
+    done = final[...].astype(F32).reshape(count * chunk, channels)
+    for i in range(3):
+        project_out[:, i * channels : (i + 1) * channels] = done[i * channels : (i + 1) * channels]
+    output_out[...] = done[3 * channels : used]
+    bias_out[...] = done[used : used + heads, : WIN**3]
+    gain_out[...] = done[used + 8 : used + 9]
+    every(token_copy, 1, "wait_send")
+    every(grad_copy, 1, "wait_send")
+    loop(lambda k: part_copy(k).wait_send())
+    loop(lambda k: whole_copy(k).wait_send())
 
 
 def shards(tokens, norm_gain, project_weight, output_weight, position_bias, grad_output):
     inner, channels = tokens.shape[:3], tokens.shape[3]
     heads = position_bias.shape[0]
-    sizes = tuple(lax.axis_size(axis) for axis in ("gx", "gy", "gz"))
+    sizes = tuple(lax.axis_size(axis) for axis in AXES)
     dims = tuple(size + 2 * RADIUS for size in inner)
     rows = inner[0] * inner[1] * inner[2]
-    count = dims[0] * dims[1] * dims[2]
-    lanes = -(-count // 128) * 128
-    factor = (rows * sizes[0] * sizes[1] * sizes[2]) ** (-0.5)
-    padded = with_halo(tokens, (("gx", 0), ("gy", 1), ("gz", 2)), RADIUS)
-    padded = jnp.pad(padded.astype(F32).reshape(count, channels), ((0, lanes - count), (0, 0)))
-    d_hidden, d_hidden_l, sums = pl.pallas_call(
-        functools.partial(kernel, inner, dims, sizes),
+    lanes = -(-dims[0] * dims[1] * dims[2] // 128) * 128
+    count = sizes[0] * sizes[1] * sizes[2]
+    factor = (rows * count) ** (-0.5)
+    chunk = -(-(4 * channels + 16) // (16 * count)) * 16
+    tile = inner[0] * inner[1] * RADIUS
+    vmem = pl.BlockSpec(memory_space=pltpu.VMEM)
+    many = len(TURNS)
+    out = pl.pallas_call(
+        functools.partial(kernel, inner, dims, sizes, factor, chunk),
         out_shape=(
-            jax.ShapeDtypeStruct((lanes, channels), F32),
-            jax.ShapeDtypeStruct((rows, channels), F32),
-            jax.ShapeDtypeStruct((4 * channels + 16, channels), F32),
+            jax.ShapeDtypeStruct(tokens.shape, F32),
+            jax.ShapeDtypeStruct((channels, 3 * channels), F32),
+            jax.ShapeDtypeStruct((channels, channels), F32),
+            jax.ShapeDtypeStruct((1, channels), F32),
+            jax.ShapeDtypeStruct(position_bias.shape, F32),
         ),
-        in_specs=[pl.BlockSpec(memory_space=pltpu.VMEM)] * 7,
-        out_specs=(pl.BlockSpec(memory_space=pltpu.VMEM),) * 3,
+        in_specs=[vmem] * 6,
+        out_specs=(vmem,) * 5,
         scratch_shapes=[
             pltpu.VMEM((heads * rows, lanes), F32),
             pltpu.VMEM((heads * rows, lanes), BF),
             pltpu.VMEM((heads * rows, lanes), BF),
             pltpu.VMEM((8, 128), F32),
-        ],
-        compiler_params=pltpu.CompilerParams(vmem_limit_bytes=40 * 2**20),
+            pltpu.VMEM((2, tile, channels), F32),
+            pltpu.VMEM((2, tile, channels), BF),
+            pltpu.VMEM((dims[0], dims[1], inner[2], channels), BF),
+            pltpu.VMEM((len(EDGES), tile, channels), BF),
+            pltpu.VMEM((lanes, channels), F32),
+            pltpu.VMEM((lanes, channels), F32),
+            pltpu.VMEM((len(EDGES), tile, channels), F32),
+            pltpu.VMEM((dims[0], dims[1], inner[2], channels), BF),
+            pltpu.VMEM((len(EDGES), tile, channels), BF),
+            pltpu.VMEM((len(FLAT),) + inner + (channels,), BF),
+            pltpu.VMEM((len(EDGES), tile, channels), BF),
+            pltpu.VMEM((count * chunk, channels), F32),
+            pltpu.VMEM((count, chunk, channels), BF),
+            pltpu.VMEM((count, chunk, channels), BF),
+            pltpu.VMEM((count, chunk, channels), BF),
+        ]
+        + [pltpu.SemaphoreType.DMA((many,))] * 4
+        + [pltpu.SemaphoreType.DMA((count,))] * 4,
+        compiler_params=pltpu.CompilerParams(
+            vmem_limit_bytes=40 * 2**20, collective_id=0, has_side_effects=True
+        ),
     )(
-        padded,
-        tokens.reshape(rows, channels),
+        tokens,
         norm_gain.reshape(1, channels),
         project_weight,
         output_weight,
         position_bias,
         grad_output.reshape(rows, channels),
     )
-    summed = lax.psum(sums, ("gx", "gy", "gz")) * factor
-    grid = d_hidden[:count].reshape(dims + (channels,))
-    mine = fold_halo(grid, (("gz", 2), ("gy", 1), ("gx", 0)), RADIUS).reshape(rows, channels)
-    d_scaled = (mine + d_hidden_l) * norm_gain
-    x = tokens.reshape(rows, channels).astype(F32)
-    inverse = lax.rsqrt(jnp.mean(x * x, axis=-1, keepdims=True) + 1e-06)
-    scaled = x * inverse
-    token_grad = inverse * (d_scaled - scaled * jnp.mean(d_scaled * scaled, axis=-1, keepdims=True))
-    project_grad = jnp.concatenate(
-        [summed[i * channels : (i + 1) * channels] for i in range(3)], axis=1
-    )
-    return (
-        token_grad.reshape(tokens.shape),
-        project_grad,
-        summed[3 * channels : 4 * channels],
-        summed[4 * channels + 8],
-        summed[4 * channels : 4 * channels + heads, : WIN**3],
-    )
+    token_grad, project_grad, output_grad, gain_grad, bias_grad = out
+    return token_grad, project_grad, output_grad, gain_grad.reshape(channels), bias_grad
 
 
 def solution(mesh):

time: 153 us -> 37.1 us (0.24)
  waiting for transfers between devices: 94.7 us -> 0 us
  starting transfers between devices: 30.3 us -> 0 us
  Pallas kernels: 7.19 us -> 29.2 us
  between operations: 14.3 us -> 0.66 us
  local copies, waits for them, and re-layouts: 2.87 us -> 6.86 us
  other arithmetic: 3.05 us -> 0 us
    psum x1 -> x0, waiting for transfers between devices: 81.7 us -> none  [shards(): summed = lax.psum(sums, ('gx', 'gy', 'gz')) * factor]
    ppermute x12 -> x0, starting transfers between devices: 30.3 us -> none  [the longest x3 12.9 us: fold_halo(): lax.ppermute(lax.slice_in_dim(array, length - width, length, axis=dim), a...]
    pallas_call x1, Pallas kernels: 7.19 us -> 29.2 us  [shards(): pl.pallas_call(functools.partial(kernel, inner, dims, sizes, factor, chun...]
    ppermute x12 -> x0, waiting for transfers between devices: 13 us -> none  [the longest x3 10 us: with_halo(): after = lax.ppermute(leading, axis, down)]
    unnamed x14 -> x17, local copies, waits for them, and re-layouts: 0.84 us -> 6.86 us
    mul x2 -> x0, other arithmetic: 1.72 us -> none  [the longest x1 0.98 us: shards(): summed = lax.psum(sums, ('gx', 'gy', 'gz')) * factor]
  transfers between devices with their start and end apart: 13 -> 0, of which waited for: 8 -> 0; matrix products, arithmetic and copies ran while one was open for 2% -> 0% of each run, Pallas kernels for 0% -> 0%
where the time goes in v2:
time: 37.1 us; the launch traced here: 36.7 us
  Pallas kernels  29.2 us (79%)
  local copies, waits for them, and re-layouts  6.86 us (18%)
  between operations  0.66 us (2%)
    pallas_call x1, Pallas kernels, shards(): pl.pallas_call(functools.partial(kernel, inner, dims, sizes, factor, chun...  29.2 us
    unnamed x17, local copies, waits for them, and re-layouts  6.86 us

profile of v2, /device:TPU:0, one launch (start us, length us, event | category | flops | bytes accessed | tf_op | source)
XLA Modules:
  0.0 36.7 jit_solution(1866619951224079)
XLA Ops:
  0.6 0.0 copy-start.4
  0.6 0.0 copy-start.5
  0.7 0.7 %copy-done.4 = f32[4,125]{1,0:T(4,128)S(1)} copy-done((f32[4,125]{1,0:T(4,128)S(1)}, f32[4,125]{1,0:T(4,128)}, u32[]{:S(2)}) %copy-start.4) | copy-done | bytes 2024
  1.3 0.0 copy-done.5
  1.3 0.0 copy-start
  1.3 0.9 %copy-done = bf16[128,384]{1,0:T(8,128)(2,1)S(1)} copy-done((bf16[128,384]{1,0:T(8,128)(2,1)S(1)}, bf16[128,384]{1,0:T(8,128)(2,1)}, u32[]{:S(2)}) %copy-start) | copy-done | bytes 98328
  2.2 0.0 copy-start.1
  2.2 0.8 %copy-done.1 = bf16[2,4,16,128]{3,2,1,0:T(8,128)(2,1)S(1)} copy-done((bf16[2,4,16,128]{3,2,1,0:T(8,128)(2,1)S(1)}, bf16[2,4,16,128]{3,2,1,0:T(8,128)(2,1)}, u32[]{:S(2)}) %copy-start.1) | copy-done | bytes 32792
  3.0 0.0 copy-start.2
  3.0 0.8 %copy-done.2 = bf16[128,128]{1,0:T(8,128)(2,1)S(1)} copy-done((bf16[128,128]{1,0:T(8,128)(2,1)S(1)}, bf16[128,128]{1,0:T(8,128)(2,1)}, u32[]{:S(2)}) %copy-start.2) | copy-done | bytes 32792
  3.7 0.0 copy-start.3
  3.7 0.8 %copy-done.3 = bf16[2,4,16,128]{3,2,1,0:T(8,128)(2,1)S(1)} copy-done((bf16[2,4,16,128]{3,2,1,0:T(8,128)(2,1)S(1)}, bf16[2,4,16,128]{3,2,1,0:T(8,128)(2,1)}, u32[]{:S(2)}) %copy-start.3) | copy-done | bytes 32792
  4.5 29.2 %shard_map.101 = (f32[2,4,16,128]{3,2,1,0:T(8,128)S(1)}, f32[128,384]{1,0:T(8,128)S(1)}, f32[128,128]{1,0:T(8,128)S(1)}, f32[1,128]{1,0:T(1,128)S(1)}, f32[4,125]{1,0:T(4,128)S(1)}) custom-call(bf16[2,4,16,128]{3,2,1,0:T(8,128)(2,1)S(1)} %copy-done.1, f32[1,128]{1,0:T(1,128)S(1)} %bitcast.4, bf16[128,384]{1,0:T(8,128)(2,1)S(1)} %copy-done, ...), custom_call_target="tpu_custom_call" | custom-call | tf_op jit(solution)/shard_map/pallas_call | solution.py:421
  33.7 0.6 %copy.16 = f32[2,4,16,128]{3,2,1,0:T(8,128)} copy(f32[2,4,16,128]{3,2,1,0:T(8,128)S(1)} %get-tuple-element.20) | data formatting | bytes 131072
  34.3 0.7 %copy.17 = f32[128,384]{1,0:T(8,128)} copy(f32[128,384]{1,0:T(8,128)S(1)} %get-tuple-element.21) | data formatting | bytes 393216
  35.0 0.6 %copy.18 = f32[128,128]{1,0:T(8,128)} copy(f32[128,128]{1,0:T(8,128)S(1)} %get-tuple-element.22) | data formatting | bytes 131072
  35.6 0.5 %copy.19 = f32[128]{0:T(128)} copy(f32[128]{0:T(128)S(1)} %bitcast.5) | data formatting | bytes 1024
  36.1 0.6 %copy.20 = f32[4,125]{1,0:T(4,128)} copy(f32[4,125]{1,0:T(4,128)S(1)} %get-tuple-element.24) | data formatting | bytes 4000
Async XLA Ops:
  0.6 0.7 %copy-start.4 = (f32[4,125]{1,0:T(4,128)S(1)}, f32[4,125]{1,0:T(4,128)}, u32[]{:S(2)}) copy-start(f32[4,125]{1,0:T(4,128)} %bias_ref.1) | copy-start | bytes 6004
  0.6 0.7 %copy-start.5 = (f32[128]{0:T(128)S(1)}, f32[128]{0:T(128)}, u32[]{:S(2)}) copy-start(f32[128]{0:T(128)} %param.7) | copy-start | bytes 1540
  1.3 0.9 %copy-start = (bf16[128,384]{1,0:T(8,128)(2,1)S(1)}, bf16[128,384]{1,0:T(8,128)(2,1)}, u32[]{:S(2)}) copy-start(bf16[128,384]{1,0:T(8,128)(2,1)} %project_ref.1) | copy-start | bytes 294916
  2.2 0.8 %copy-start.1 = (bf16[2,4,16,128]{3,2,1,0:T(8,128)(2,1)S(1)}, bf16[2,4,16,128]{3,2,1,0:T(8,128)(2,1)}, u32[]{:S(2)}) copy-start(bf16[2,4,16,128]{3,2,1,0:T(8,128)(2,1)} %tokens_ref.1) | copy-start | bytes 98308
  3.0 0.8 %copy-start.2 = (bf16[128,128]{1,0:T(8,128)(2,1)S(1)}, bf16[128,128]{1,0:T(8,128)(2,1)}, u32[]{:S(2)}) copy-start(bf16[128,128]{1,0:T(8,128)(2,1)} %output_ref.1) | copy-start | bytes 98308
  3.7 0.8 %copy-start.3 = (bf16[2,4,16,128]{3,2,1,0:T(8,128)(2,1)S(1)}, bf16[2,4,16,128]{3,2,1,0:T(8,128)(2,1)}, u32[]{:S(2)}) copy-start(bf16[2,4,16,128]{3,2,1,0:T(8,128)(2,1)} %param.11) | copy-start | bytes 98308

commit v3 on v2

--- a/solution.py
+++ b/solution.py
@@ -190,13 +190,23 @@
 
 def kernel(
     inner, dims, sizes, factor, chunk,
-    tokens_ref, gain_ref, project_ref, output_ref, bias_ref, go_ref,
+    tokens_hbm, gain_hbm, project_hbm, output_hbm, bias_hbm, go_hbm,
     token_out, project_out, output_out, gain_out, bias_out,
     table, probs_s, low_s, spread,
     edge_f, edge, main, rims, padded, hidden_f, pack_f, out_main, out_edge, in_main, in_edge,
     sums_f, sums, parts, final,
-    tok_send, tok_recv, ret_send, ret_recv, rs_send, rs_recv, ag_send, ag_recv,
+    tokens_ref, gain_ref, project_ref, output_ref, bias_ref, go_ref,
+    tok_send, tok_recv, ret_send, ret_recv, rs_send, rs_recv, ag_send, ag_recv, in_sem,
 ):
+    fetches = [
+        pltpu.make_async_copy(source, target, in_sem.at[n])
+        for n, (source, target) in enumerate((
+            (tokens_hbm, tokens_ref), (bias_hbm, bias_ref), (gain_hbm, gain_ref),
+            (project_hbm, project_ref), (output_hbm, output_ref), (go_hbm, go_ref),
+        ))
+    ]
+    for fetch in fetches:
+        fetch.start()
     size_x, size_y, size_z = inner
     pad_x, pad_y, pad_z = dims
     rows = size_x * size_y * size_z
@@ -234,6 +244,7 @@
         return carry
 
     lax.fori_loop(1, count, greet, 0)
+    fetches[0].wait()
     for x in range(size_x):
         for y in range(size_y):
             line = tokens_ref[x, y].astype(F32)
@@ -276,10 +287,13 @@
             pl.when(exists(turn, sign))(lambda turn=turn: getattr(make(turn), what)())
 
     every(token_copy, 1, "start")
+    fetches[1].wait()
     bias_table(
         bias_ref, spread, table, inner, dims, lanes,
         [(at, size * cells) for at, size, cells in zip(here, sizes, inner)],
     )
+    for fetch in fetches[2:]:
+        fetch.wait()
     every(token_copy, -1, "wait_recv")
 
     filled = pad_x * pad_y * pad_z
@@ -323,20 +337,27 @@
         send_hidden,
     )
     used = 4 * channels
-    for i in range(3):
-        sums_f[i * channels : (i + 1) * channels, :] = project[i]
-    sums_f[3 * channels : used, :] = output
-    sums_f[used : used + 8, :] = bias_sum
-    sums_f[used + 8 : used + 16, :] = jnp.broadcast_to(gain_sum, (8, channels))
-    if count * chunk > used + 16:
-        sums_f[used + 16 :, :] = jnp.zeros((count * chunk - used - 16, channels), F32)
-    sums[...] = sums_f[...].astype(BF).reshape(count, chunk, channels)
+    blocks = project + (output,)
+    full = jnp.concatenate(blocks, axis=0).astype(BF)
+    if count * chunk > used:
+        full = jnp.concatenate([full, jnp.zeros((count * chunk - used, channels), BF)], axis=0)
+    sums[:, 0:chunk, :] = full.reshape(count, chunk, channels)
+    sums_f[0:8, :] = bias_sum
+    sums_f[8:16, :] = jnp.broadcast_to(gain_sum, (8, channels))
+    sums[:, chunk:, :] = jnp.broadcast_to(sums_f[...].astype(BF)[None], (count, 16, channels))
 
     def part_copy(k):
         other, place = peer(k)
         return pltpu.make_async_remote_copy(
-            src_ref=sums.at[other], dst_ref=parts.at[k], send_sem=rs_send.at[k],
+            src_ref=sums.at[other], dst_ref=parts.at[me], send_sem=rs_send.at[k],
             recv_sem=rs_recv.at[k], device_id=place, device_id_type=MESH,
+        )
+
+    def part_arrival(k):
+        other = lax.rem(me + count - k, count)
+        return pltpu.make_async_remote_copy(
+            src_ref=sums.at[other], dst_ref=parts.at[other], send_sem=rs_send.at[k],
+            recv_sem=rs_recv.at[k], device_id=peer(k)[1], device_id_type=MESH,
         )
 
     def whole_copy(k):
@@ -357,6 +378,7 @@
         lax.fori_loop(1, count, lambda k, carry: (body(k), carry)[1], 0)
 
     loop(lambda k: part_copy(k).start())
+    parts[me] = sums[me]
 
     every(grad_copy, -1, "wait_recv")
     norm_scaled = d_hidden_l
@@ -386,23 +408,36 @@
     )
     token_out[...] = token_grad.reshape(inner + (channels,))
 
-    loop(lambda k: part_copy(k).wait_recv())
+    loop(lambda k: part_arrival(k).wait_recv())
     total = lax.fori_loop(
-        1, count, lambda k, carry: carry + parts[k].astype(F32), sums[me].astype(F32)
-    )
-    final[me] = (total * factor).astype(BF)
+        1, count, lambda k, carry: carry + parts[k].astype(F32), parts[0].astype(F32)
+    ) * factor
+    final[me] = total[0:chunk].astype(BF)
     loop(lambda k: whole_copy(k).start())
     loop(lambda k: whole_arrival(k).wait_recv())
     done = final[...].astype(F32).reshape(count * chunk, channels)
     for i in range(3):
         project_out[:, i * channels : (i + 1) * channels] = done[i * channels : (i + 1) * channels]
     output_out[...] = done[3 * channels : used]
-    bias_out[...] = done[used : used + heads, : WIN**3]
-    gain_out[...] = done[used + 8 : used + 9]
+    bias_out[...] = total[chunk : chunk + heads, : WIN**3]
+    gain_out[...] = total[chunk + 8 : chunk + 9]
     every(token_copy, 1, "wait_send")
     every(grad_copy, 1, "wait_send")
     loop(lambda k: part_copy(k).wait_send())
     loop(lambda k: whole_copy(k).wait_send())
+
+
+def write_out(*refs):
+    sources, targets, sem = list(refs[:5]), refs[5:10], refs[10]
+    sources[3] = sources[3].at[0]
+    copies = [
+        pltpu.make_async_copy(source, target, sem.at[n])
+        for n, (source, target) in enumerate(zip(sources, targets))
+    ]
+    for copy in copies:
+        copy.start()
+    for copy in copies:
+        copy.wait()
 
 
 def shards(tokens, norm_gain, project_weight, output_weight, position_bias, grad_output):
@@ -414,7 +449,7 @@
     lanes = -(-dims[0] * dims[1] * dims[2] // 128) * 128
     count = sizes[0] * sizes[1] * sizes[2]
     factor = (rows * count) ** (-0.5)
-    chunk = -(-(4 * channels + 16) // (16 * count)) * 16
+    chunk = -(-4 * channels // (16 * count)) * 16
     tile = inner[0] * inner[1] * RADIUS
     vmem = pl.BlockSpec(memory_space=pltpu.VMEM)
     many = len(TURNS)
@@ -427,7 +462,7 @@
             jax.ShapeDtypeStruct((1, channels), F32),
             jax.ShapeDtypeStruct(position_bias.shape, F32),
         ),
-        in_specs=[vmem] * 6,
+        in_specs=[pl.BlockSpec(memory_space=pltpu.HBM)] * 6,
         out_specs=(vmem,) * 5,
         scratch_shapes=[
             pltpu.VMEM((heads * rows, lanes), F32),
@@ -445,15 +480,22 @@
             pltpu.VMEM((len(EDGES), tile, channels), BF),
             pltpu.VMEM((len(FLAT),) + inner + (channels,), BF),
             pltpu.VMEM((len(EDGES), tile, channels), BF),
-            pltpu.VMEM((count * chunk, channels), F32),
+            pltpu.VMEM((16, channels), F32),
+            pltpu.VMEM((count, chunk + 16, channels), BF),
+            pltpu.VMEM((count, chunk + 16, channels), BF),
             pltpu.VMEM((count, chunk, channels), BF),
-            pltpu.VMEM((count, chunk, channels), BF),
-            pltpu.VMEM((count, chunk, channels), BF),
+            pltpu.VMEM(tokens.shape, BF),
+            pltpu.VMEM((1, channels), F32),
+            pltpu.VMEM(project_weight.shape, BF),
+            pltpu.VMEM(output_weight.shape, BF),
+            pltpu.VMEM(position_bias.shape, F32),
+            pltpu.VMEM((rows, channels), BF),
         ]
         + [pltpu.SemaphoreType.DMA((many,))] * 4
-        + [pltpu.SemaphoreType.DMA((count,))] * 4,
+        + [pltpu.SemaphoreType.DMA((count,))] * 4
+        + [pltpu.SemaphoreType.DMA((6,))],
         compiler_params=pltpu.CompilerParams(
-            vmem_limit_bytes=40 * 2**20, collective_id=0, has_side_effects=True
+            vmem_limit_bytes=62 * 2**20, collective_id=0, has_side_effects=True
         ),
     )(
         tokens,
@@ -463,8 +505,18 @@
         position_bias,
         grad_output.reshape(rows, channels),
     )
-    token_grad, project_grad, output_grad, gain_grad, bias_grad = out
-    return token_grad, project_grad, output_grad, gain_grad.reshape(channels), bias_grad
+    results = pl.pallas_call(
+        write_out,
+        out_shape=tuple(
+            jax.ShapeDtypeStruct((channels,) if n == 3 else part.shape, F32)
+            for n, part in enumerate(out)
+        ),
+        in_specs=[pl.BlockSpec(memory_space=pltpu.HBM)] * 5,
+        out_specs=(pl.BlockSpec(memory_space=pltpu.HBM),) * 5,
+        scratch_shapes=[pltpu.SemaphoreType.DMA((5,))],
+        compiler_params=pltpu.CompilerParams(vmem_limit_bytes=62 * 2**20),
+    )(*out)
+    return tuple(results)
 
 
 def solution(mesh):

time: 37.1 us -> 41.8 us (1.13)
  Pallas kernels: 29.2 us -> 41 us
  local copies, waits for them, and re-layouts: 6.86 us -> 0 us
    pallas_call x0 -> x1, Pallas kernels: none -> 11.2 us  [shards(): pl.pallas_call(write_out, out_shape=tuple((jax.ShapeDtypeStruct((channels...]
    unnamed x17 -> x0, local copies, waits for them, and re-layouts: 6.86 us -> none
    pallas_call x1, Pallas kernels: 29.2 us -> 29.8 us  [shards(): pl.pallas_call(functools.partial(kernel, inner, dims, sizes, factor, chun...]
where the time goes in v3:
time: 41.8 us; the launch traced here: 41.6 us
  Pallas kernels  41 us (98%)
  between operations  0.64 us (2%)
    pallas_call x1, Pallas kernels, shards(): pl.pallas_call(functools.partial(kernel, inner, dims, sizes, factor, chun...  29.8 us
    pallas_call x1, Pallas kernels, shards(): pl.pallas_call(write_out, out_shape=tuple((jax.ShapeDtypeStruct((channels...  11.2 us

profile of v3, /device:TPU:0, one launch (start us, length us, event | category | flops | bytes accessed | tf_op | source)
XLA Modules:
  0.0 41.6 jit_solution(12929248450483794375)
XLA Ops:
  0.6 29.8 %shard_map.101 = (f32[2,4,16,128]{3,2,1,0:T(8,128)}, f32[128,384]{1,0:T(8,128)}, f32[128,128]{1,0:T(8,128)}, f32[1,128]{1,0:T(1,128)}, f32[4,125]{1,0:T(4,128)}) custom-call(bf16[2,4,16,128]{3,2,1,0:T(8,128)(2,1)} %tokens_hbm.1, f32[1,128]{1,0:T(1,128)} %bitcast.3, bf16[128,384]{1,0:T(8,128)(2,1)} %project_hbm.1, bf16[128,128]{1,0:T(8,128)(2,1)} %output_hbm.1, ...), custom_call_target="tpu_custom_call" | custom-call | tf_op jit(solution)/shard_map/pallas_call | solution.py:456
  30.5 11.2 %shard_map.102 = (f32[2,4,16,128]{3,2,1,0:T(8,128)}, f32[128,384]{1,0:T(8,128)}, f32[128,128]{1,0:T(8,128)}, f32[128]{0:T(128)}, f32[4,125]{1,0:T(4,128)}) custom-call(f32[2,4,16,128]{3,2,1,0:T(8,128)} %get-tuple-element.10.refs_0_, f32[128,384]{1,0:T(8,128)} %get-tuple-element.11.refs_1_, f32[128,128]{1,0:T(8,128)} %get-tuple-element.12.refs_2_, ...), custom_call_target="tpu_custom_call" | custom-call | tf_op jit(solution)/shard_map/pallas_call | solution.py:508

commit v4 on v3

--- a/solution.py
+++ b/solution.py
@@ -428,15 +428,18 @@
 
 
 def write_out(*refs):
-    sources, targets, sem = list(refs[:5]), refs[5:10], refs[10]
-    sources[3] = sources[3].at[0]
-    copies = [
-        pltpu.make_async_copy(source, target, sem.at[n])
-        for n, (source, target) in enumerate(zip(sources, targets))
+    sources, targets, held, in_sem, out_sem = refs[:5], list(refs[5:10]), refs[10:15], refs[15], refs[16]
+    takes = [pltpu.make_async_copy(sources[n], held[n], in_sem.at[n]) for n in range(5)]
+    gives = [
+        pltpu.make_async_copy(held[n].at[0] if n == 3 else held[n], targets[n], out_sem.at[n])
+        for n in range(5)
     ]
-    for copy in copies:
+    for copy in takes:
         copy.start()
-    for copy in copies:
+    for take, give in zip(takes, gives):
+        take.wait()
+        give.start()
+    for copy in gives:
         copy.wait()
 
 
@@ -513,7 +516,8 @@
         ),
         in_specs=[pl.BlockSpec(memory_space=pltpu.HBM)] * 5,
         out_specs=(pl.BlockSpec(memory_space=pltpu.HBM),) * 5,
-        scratch_shapes=[pltpu.SemaphoreType.DMA((5,))],
+        scratch_shapes=[pltpu.VMEM(part.shape, F32) for part in out]
+        + [pltpu.SemaphoreType.DMA((5,))] * 2,
         compiler_params=pltpu.CompilerParams(vmem_limit_bytes=62 * 2**20),
     )(*out)
     return tuple(results)

time: 41.8 us -> 32.4 us (0.78)
  Pallas kernels: 41 us -> 31.6 us
    pallas_call x1, Pallas kernels: 11.2 us -> 1.75 us  [shards(): pl.pallas_call(write_out, out_shape=tuple((jax.ShapeDtypeStruct((channels...]
where the time goes in v4:
time: 32.4 us; the launch traced here: 32.2 us
  Pallas kernels  31.6 us (98%)
  between operations  0.64 us (2%)
    pallas_call x1, Pallas kernels, shards(): pl.pallas_call(functools.partial(kernel, inner, dims, sizes, factor, chun...  29.8 us
    pallas_call x1, Pallas kernels, shards(): pl.pallas_call(write_out, out_shape=tuple((jax.ShapeDtypeStruct((channels...  1.75 us

profile of v4, /device:TPU:0, one launch (start us, length us, event | category | flops | bytes accessed | tf_op | source)
XLA Modules:
  0.0 32.2 jit_solution(12657598902877675080)
XLA Ops:
  0.6 29.8 %shard_map.101 = (f32[2,4,16,128]{3,2,1,0:T(8,128)}, f32[128,384]{1,0:T(8,128)}, f32[128,128]{1,0:T(8,128)}, f32[1,128]{1,0:T(1,128)}, f32[4,125]{1,0:T(4,128)}) custom-call(bf16[2,4,16,128]{3,2,1,0:T(8,128)(2,1)} %tokens_hbm.1, f32[1,128]{1,0:T(1,128)} %bitcast.3, bf16[128,384]{1,0:T(8,128)(2,1)} %project_hbm.1, bf16[128,128]{1,0:T(8,128)(2,1)} %output_hbm.1, ...), custom_call_target="tpu_custom_call" | custom-call | tf_op jit(solution)/shard_map/pallas_call | solution.py:459
  30.5 1.8 %shard_map.102 = (f32[2,4,16,128]{3,2,1,0:T(8,128)}, f32[128,384]{1,0:T(8,128)}, f32[128,128]{1,0:T(8,128)}, f32[128]{0:T(128)}, f32[4,125]{1,0:T(4,128)}) custom-call(f32[2,4,16,128]{3,2,1,0:T(8,128)} %get-tuple-element.10.refs_0_, f32[128,384]{1,0:T(8,128)} %get-tuple-element.11.refs_1_, f32[128,128]{1,0:T(8,128)} %get-tuple-element.12.refs_2_, ...), custom_call_target="tpu_custom_call" | custom-call | tf_op jit(solution)/shard_map/pallas_call | solution.py:511

commit v5 on v4

--- a/solution.py
+++ b/solution.py
@@ -243,7 +243,7 @@
         pl.semaphore_signal(barrier, inc=1, device_id=peer(k)[1], device_id_type=MESH)
         return carry
 
-    lax.fori_loop(1, count, greet, 0)
+    lax.fori_loop(1, count, greet, 0, unroll=count <= 32)
     fetches[0].wait()
     for x in range(size_x):
         for y in range(size_y):
@@ -375,7 +375,7 @@
         )
 
     def loop(body):
-        lax.fori_loop(1, count, lambda k, carry: (body(k), carry)[1], 0)
+        lax.fori_loop(1, count, lambda k, carry: (body(k), carry)[1], 0, unroll=count <= 32)
 
     loop(lambda k: part_copy(k).start())
     parts[me] = sums[me]

time: 32.4 us -> 32.1 us (level)
  no operation moved by 1% of the time
where the time goes in v5:
time: 32.1 us; the launch traced here: 32 us
  Pallas kernels  31.3 us (98%)
  between operations  0.64 us (2%)
    pallas_call x1, Pallas kernels, shards(): pl.pallas_call(functools.partial(kernel, inner, dims, sizes, factor, chun...  29.6 us
    pallas_call x1, Pallas kernels, shards(): pl.pallas_call(write_out, out_shape=tuple((jax.ShapeDtypeStruct((channels...  1.75 us

profile of v5, /device:TPU:0, one launch (start us, length us, event | category | flops | bytes accessed | tf_op | source)
XLA Modules:
  0.0 32.0 jit_solution(7444344169716798997)
XLA Ops:
  0.6 29.6 %shard_map.101 = (f32[2,4,16,128]{3,2,1,0:T(8,128)}, f32[128,384]{1,0:T(8,128)}, f32[128,128]{1,0:T(8,128)}, f32[1,128]{1,0:T(1,128)}, f32[4,125]{1,0:T(4,128)}) custom-call(bf16[2,4,16,128]{3,2,1,0:T(8,128)(2,1)} %tokens_hbm.1, f32[1,128]{1,0:T(1,128)} %bitcast.3, bf16[128,384]{1,0:T(8,128)(2,1)} %project_hbm.1, bf16[128,128]{1,0:T(8,128)(2,1)} %output_hbm.1, ...), custom_call_target="tpu_custom_call" | custom-call | tf_op jit(solution)/shard_map/pallas_call | solution.py:459
  30.2 1.8 %shard_map.102 = (f32[2,4,16,128]{3,2,1,0:T(8,128)}, f32[128,384]{1,0:T(8,128)}, f32[128,128]{1,0:T(8,128)}, f32[128]{0:T(128)}, f32[4,125]{1,0:T(4,128)}) custom-call(f32[2,4,16,128]{3,2,1,0:T(8,128)} %get-tuple-element.10.refs_0_, f32[128,384]{1,0:T(8,128)} %get-tuple-element.11.refs_1_, f32[128,128]{1,0:T(8,128)} %get-tuple-element.12.refs_2_, ...), custom_call_target="tpu_custom_call" | custom-call | tf_op jit(solution)/shard_map/pallas_call | solution.py:511
